TPU v7x, 128 devices: a whole 4x4x4 slice. The times are simulated.
128 devices in a mesh: row: 8 (over y, x_lo), col: 16 (over x_hi, z, core).
Axes of the slice: x: 4 (x_hi: 2, x_lo: 2; x = x_hi * 2 + x_lo), y: 4, z: 4, core: 2. Of those that a mesh axis runs over, the one named last changes fastest.
Arguments:
- points: bfloat16 [1048576, 256], P(('row', 'col')), may hold values from -6 to 6
- leaf_bases: bfloat16 [1048576, 128], P(('row', 'col')), may hold values from -0.25 to 0.25
- own_maps: bfloat16 [4, 2048, 128, 128], P(None, ('row', 'col')), may hold values from -0.375 to 0.375
- partner_maps: bfloat16 [4, 2048, 128, 128], P(None, ('row', 'col')), may hold values from -0.375 to 0.375
- expand_bases: bfloat16 [1048576, 128], P(('row', 'col')), may hold values from -0.5 to 0.5
- ranks: int32 [5, 2048], P(None, ('row', 'col')), may hold values from 64 to 128
Outputs:
- scattered: bfloat16 [1048576, 256], P(('row', 'col'))
All inputs are finite; a program needn't handle non-finite values.
Results may differ from a plain program's by a relative error of at most 0.009.
Values may be sent and summed in bfloat16 or wider, within the bound.
No kernel may reach another device: no remote copies, remote signals or barrier semaphores. Data moves between devices by JAX's collectives and lax.ppermute only.
A program may use at most 64 MiB of HBM per device.

v0:
```python
import jax
import jax.numpy as jnp
from jax import lax
from jax.sharding import PartitionSpec as P

LEAF = 512


def swapped(block, axis, apart):
    count = lax.axis_size(axis)
    route = []
    for low in range(count):
        high = low | 1 << apart
        if high != low and high < count:
            route += [(low, high), (high, low)]
    return lax.ppermute(block, axis, route)


def advance(state, other, own, partner, keep):
    mixed = jnp.einsum("bij,bjr->bir", own, state, preferred_element_type=jnp.float32)
    mixed = mixed + jnp.einsum("bij,bjr->bir", partner, other, preferred_element_type=jnp.float32)
    return (mixed * keep).astype(jnp.bfloat16)


def on_device(points, leaf_bases, own_maps, partner_maps, expand_bases, ranks):
    p_dev, rhs = points.shape
    rank_max = leaf_bases.shape[1]
    row_size = lax.axis_size("row")
    col_size = lax.axis_size("col")
    moved = lax.all_to_all(points, ("row", "col"), split_axis=0, concat_axis=0, tiled=True)
    blocks = p_dev // LEAF
    columns = jnp.arange(rank_max, dtype=jnp.int32)
    keep = (columns[None, None, :] < ranks[:, :, None]).astype(jnp.float32)[..., None]
    coeff = jnp.einsum(
        "blk,blr->bkr",
        leaf_bases.reshape(blocks, LEAF, rank_max),
        moved.reshape(blocks, LEAF, rhs),
        preferred_element_type=jnp.float32,
    )
    state = (coeff * keep[0]).astype(jnp.bfloat16)
    col_bits = col_size.bit_length() - 1
    row_bits = row_size.bit_length() - 1
    for level in range(3):
        bit_index = col_bits - 1 - level
        other = swapped(state, "col", bit_index)
        state = advance(state, other, own_maps[level], partner_maps[level], keep[level + 1])
    other = swapped(state, "row", row_bits - 1)
    state = advance(state, other, own_maps[3], partner_maps[3], keep[4])
    result = jnp.einsum(
        "blk,bkr->blr",
        expand_bases.reshape(blocks, LEAF, rank_max),
        state,
        preferred_element_type=jnp.float32,
    )
    return result.astype(jnp.bfloat16).reshape(p_dev, rhs)


def solution(mesh):
    return jax.shard_map(
        on_device,
        mesh=mesh,
        in_specs=(
            P(("row", "col"), None),
            P(("row", "col"), None),
            P(None, ("row", "col"), None, None),
            P(None, ("row", "col"), None, None),
            P(("row", "col"), None),
            P(None, ("row", "col")),
        ),
        out_specs=P(("row", "col"), None),
        check_vma=False,
    )
```

profile of v0, /device:TPU:2, one launch (start us, length us, event | category | flops | bytes accessed | tf_op | source)
XLA Modules:
  0.0 180.4 jit_solution(3406937323764058110)
XLA Ops:
  0.0 0.0 copy-start
  0.0 0.0 copy-start.3
  0.0 11.0 %all-to-all-start = ((bf16[128,64,256]{2,1,0:T(8,128)(2,1)}), bf16[128,64,256]{2,1,0:T(8,128)(2,1)}, u32[]{:S(2)}, u32[]{:S(2)}) async-start(bf16[128,64,256]{2,1,0:T(8,128)(2,1)} %bitcast.57), calls=%async_computation | async-start | bytes 8388608 | tf_op jit(solution)/shard_map/all_to_all | solution.py:30
  11.0 0.0 copy-done.3
  11.0 0.1 fusion.23
  11.1 51.4 %all-to-all-done = bf16[128,64,256]{2,1,0:T(8,128)(2,1)} async-done(((bf16[128,64,256]{2,1,0:T(8,128)(2,1)}), bf16[128,64,256]{2,1,0:T(8,128)(2,1)}, u32[]{:S(2)}, u32[]{:S(2)}) %all-to-all-start) | async-done | bytes 4194336 | tf_op jit(solution)/shard_map/all_to_all | solution.py:30
  62.5 0.0 copy-start.1
  62.5 4.0 %multiply_convert_fusion.4 = bf16[16,128,256]{2,1,0:T(8,128)(2,1)S(1)} fusion(bf16[16,512,128]{2,1,0:T(8,128)(2,1)} %bitcast.61, bf16[16,512,256]{2,1,0:T(8,128)(2,1)} %bitcast.2, f32[16,128]{1,0:T(8,128)S(1)} %get-tuple-element.9), kind=kOutput, calls=%fused_computation.5 | convolution fusion | flops 537919488 | bytes 7348224 | tf_op jit(solution)/shard_map/blk,blr->bkr/dot_general | solution.py:34
  66.5 0.0 copy-start.2
  66.5 2.0 %collective-permute-start = (bf16[16,128,256]{2,1,0:T(8,128)(2,1)S(1)}, bf16[16,128,256]{2,1,0:T(8,128)(2,1)S(1)}, u32[]{:S(2)}, u32[]{:S(2)}) collective-permute-start(bf16[16,128,256]{2,1,0:T(8,128)(2,1)S(1)} %multiply_convert_fusion.4), channel_id=1, source_target_pairs={{0,8},{8,0},{1,9},{9,1},{2,10},{10,2},{3,11},{11,3},{4,12},{12,4},... | collective-permute-start | bytes 3145736 | tf_op jit(solution)/shard_map/ppermute | solution.py:16
  68.5 0.0 copy-done.1
  68.5 0.5 fusion.12
  69.0 24.4 %collective-permute-done = bf16[16,128,256]{2,1,0:T(8,128)(2,1)S(1)} collective-permute-done((bf16[16,128,256]{2,1,0:T(8,128)(2,1)S(1)}, bf16[16,128,256]{2,1,0:T(8,128)(2,1)S(1)}, u32[]{:S(2)}, u32[]{:S(2)}) %collective-permute-start) | collective-permute-done | bytes 1048608 | tf_op jit(solution)/shard_map/ppermute | solution.py:16
  93.4 0.0 copy-done.2
  93.4 0.5 multiply_convert_fusion.3
  93.9 0.1 collective-permute-start.1
  94.0 0.4 fusion.9
  94.5 25.5 %collective-permute-done.1 = bf16[16,128,256]{1,2,0:T(8,128)(2,1)S(1)} collective-permute-done((bf16[16,128,256]{1,2,0:T(8,128)(2,1)S(1)}, bf16[16,128,256]{1,2,0:T(8,128)(2,1)S(1)}, u32[]{:S(2)}, u32[]{:S(2)}) %collective-permute-start.1) | collective-permute-done | bytes 1048608 | tf_op jit(solution)/shard_map/ppermute | solution.py:16
  120.0 0.4 multiply_convert_fusion.2
  120.4 0.1 collective-permute-start.2
  120.5 0.4 fusion.6
  121.0 23.1 %collective-permute-done.2 = bf16[16,128,256]{1,2,0:T(8,128)(2,1)S(1)} collective-permute-done((bf16[16,128,256]{1,2,0:T(8,128)(2,1)S(1)}, bf16[16,128,256]{1,2,0:T(8,128)(2,1)S(1)}, u32[]{:S(2)}, u32[]{:S(2)}) %collective-permute-start.2) | collective-permute-done | bytes 1048608 | tf_op jit(solution)/shard_map/ppermute | solution.py:16
  144.1 0.4 multiply_convert_fusion.1
  144.5 0.5 collective-permute-start.3
  145.0 1.8 fusion.3
  146.8 21.9 %collective-permute-done.3 = bf16[16,128,256]{1,2,0:T(8,128)(2,1)S(1)} collective-permute-done((bf16[16,128,256]{1,2,0:T(8,128)(2,1)S(1)}, bf16[16,128,256]{1,2,0:T(8,128)(2,1)S(1)}, u32[]{:S(2)}, u32[]{:S(2)}) %collective-permute-start.3) | collective-permute-done | bytes 1048608 | tf_op jit(solution)/shard_map/ppermute | solution.py:16
  168.7 0.0 copy-done
  168.7 5.2 %convert_bitcast_fusion = bf16[16,512,256]{1,2,0:T(8,128)(2,1)} fusion(bf16[16,512,128]{2,1,0:T(8,128)(2,1)S(1)} %bitcast.56, f32[16,256,128]{2,1,0:T(8,128)} %fusion.3, bf16[16,128,256]{1,2,0:T(8,128)(2,1)S(1)} %collective-permute-done.3, f32[16,128]{1,0:T(8,128)S(1)} %get-tuple-element.5, bf16[4,16,128,128]{3,2,1,0:T(8,128)(2,1)} %param.9), kind=kOutput, calls=%fused_computation | convolution fusion | flops 674758656 | bytes 9969664 | tf_op jit(solution)/shard_map/blk,bkr->blr/dot_general | solution.py:49
  174.0 6.4 %copy.13 = bf16[16,512,256]{2,1,0:T(8,128)(2,1)} copy(bf16[16,512,256]{1,2,0:T(8,128)(2,1)} %convert_bitcast_fusion) | data formatting | bytes 8388608 | tf_op jit(solution)/shard_map/convert_element_type | solution.py:55
  (1 shorter events, 0.0 us)
Async XLA Ops:
  0.0 168.7 %copy-start = (bf16[8192,128]{1,0:T(8,128)(2,1)S(1)}, bf16[8192,128]{1,0:T(8,128)(2,1)}, u32[]{:S(2)}) copy-start(bf16[8192,128]{1,0:T(8,128)(2,1)} %param.10) | copy-start | bytes 6291460
  0.0 11.0 %copy-start.3 = (s32[5,16]{1,0:T(8,128)S(1)}, s32[5,16]{1,0:T(8,128)}, u32[]{:S(2)}) copy-start(s32[5,16]{1,0:T(8,128)} %param.11) | copy-start | bytes 964
  0.0 62.5 %all-to-all-start = ((bf16[128,64,256]{2,1,0:T(8,128)(2,1)}), bf16[128,64,256]{2,1,0:T(8,128)(2,1)}, u32[]{:S(2)}, u32[]{:S(2)}) async-start(bf16[128,64,256]{2,1,0:T(8,128)(2,1)} %bitcast.57), calls=%async_computation | async-start | bytes 8388608 | tf_op jit(solution)/shard_map/all_to_all | solution.py:30
  62.5 6.0 %copy-start.1 = (bf16[4,16,128,128]{3,2,1,0:T(8,128)(2,1)S(1)}, bf16[4,16,128,128]{3,2,1,0:T(8,128)(2,1)}, u32[]{:S(2)}) copy-start(bf16[4,16,128,128]{3,2,1,0:T(8,128)(2,1)} %param.8) | copy-start | bytes 6291460
  66.5 26.9 %copy-start.2 = (bf16[4,16,128,128]{3,2,1,0:T(8,128)(2,1)S(1)}, bf16[4,16,128,128]{3,2,1,0:T(8,128)(2,1)}, u32[]{:S(2)}) copy-start(bf16[4,16,128,128]{3,2,1,0:T(8,128)(2,1)} %param.9) | copy-start | bytes 6291460
  66.5 26.9 %collective-permute-start = (bf16[16,128,256]{2,1,0:T(8,128)(2,1)S(1)}, bf16[16,128,256]{2,1,0:T(8,128)(2,1)S(1)}, u32[]{:S(2)}, u32[]{:S(2)}) collective-permute-start(bf16[16,128,256]{2,1,0:T(8,128)(2,1)S(1)} %multiply_convert_fusion.4), channel_id=1, source_target_pairs={{0,8},{8,0},{1,9},{9,1},{2,10},{10,2},{3,11},{11,3},{4,12},{12,4},... | collective-permute-start | bytes 3145736 | tf_op jit(solution)/shard_map/ppermute | solution.py:16
  93.9 26.1 %collective-permute-start.1 = (bf16[16,128,256]{1,2,0:T(8,128)(2,1)S(1)}, bf16[16,128,256]{1,2,0:T(8,128)(2,1)S(1)}, u32[]{:S(2)}, u32[]{:S(2)}) collective-permute-start(bf16[16,128,256]{1,2,0:T(8,128)(2,1)S(1)} %bitcast.58), channel_id=1, source_target_pairs={{0,4},{4,0},{1,5},{5,1},{2,6},{6,2},{3,7},{7,3},{8,12},{12,8},{9,1... | collective-permute-start | bytes 3145736 | tf_op jit(solution)/shard_map/ppermute | solution.py:16
  120.4 23.6 %collective-permute-start.2 = (bf16[16,128,256]{1,2,0:T(8,128)(2,1)S(1)}, bf16[16,128,256]{1,2,0:T(8,128)(2,1)S(1)}, u32[]{:S(2)}, u32[]{:S(2)}) collective-permute-start(bf16[16,128,256]{1,2,0:T(8,128)(2,1)S(1)} %bitcast.59), channel_id=1, source_target_pairs={{0,2},{2,0},{1,3},{3,1},{4,6},{6,4},{5,7},{7,5},{8,10},{10,8},{9,1... | collective-permute-start | bytes 3145736 | tf_op jit(solution)/shard_map/ppermute | solution.py:16
  144.5 24.2 %collective-permute-start.3 = (bf16[16,128,256]{1,2,0:T(8,128)(2,1)S(1)}, bf16[16,128,256]{1,2,0:T(8,128)(2,1)S(1)}, u32[]{:S(2)}, u32[]{:S(2)}) collective-permute-start(bf16[16,128,256]{1,2,0:T(8,128)(2,1)S(1)} %bitcast.60), channel_id=1, source_target_pairs={{0,64},{64,0},{16,80},{80,16},{32,96},{96,32},{48,112},{112,48},{1... | collective-permute-start | bytes 3145736 | tf_op jit(solution)/shard_map/ppermute | solution.py:16
where the time goes:
time: 181 us; the launch traced here: 180 us
  waiting for transfers between devices  146 us (81%)
  matrix products  13.8 us (8%)
  starting transfers between devices  13.6 us (8%)
  local copies, waits for them, and re-layouts  6.4 us (4%)
    ppermute x4, waiting for transfers between devices, swapped(): return lax.ppermute(block, axis, route)  95 us
    all_to_all x1, waiting for transfers between devices, on_device(): lax.all_to_all(points, ('row', 'col'), split_axis=0, concat_axis=0, tiled...  51.4 us
    all_to_all x1, starting transfers between devices, on_device(): lax.all_to_all(points, ('row', 'col'), split_axis=0, concat_axis=0, tiled...  11 us
    convert_element_type x1, local copies, waits for them, and re-layouts, on_device(): return result.astype(jnp.bfloat16).reshape(p_dev, rhs)  6.38 us
    dot_general x1, matrix products, on_device(): jnp.einsum('blk,bkr->blr', expand_bases.reshape(blocks, LEAF, rank_max),...  5.25 us
    dot_general x1, matrix products, on_device(): jnp.einsum('blk,blr->bkr', leaf_bases.reshape(blocks, LEAF, rank_max), mo...  3.98 us
  transfers between devices with their start and end apart: 5, of which 5 were waited for; matrix products, arithmetic and copies ran while one was open for 2% of the time, Pallas kernels for 0%

commit v1 on v0

v1 whole, which is shorter than its diff:
```python
import functools

import jax
import jax.numpy as jnp
from jax import lax
from jax.experimental import pallas as pl
from jax.experimental.pallas import tpu as pltpu
from jax.sharding import PartitionSpec as P

LEAF = 512
SIZES = [4, 4, 4, 4]
VMEM = pl.BlockSpec(memory_space=pltpu.VMEM)
ANY = pl.BlockSpec(memory_space=pl.ANY)


def swapped(block, axis, apart):
    count = lax.axis_size(axis)
    return lax.ppermute(block, axis, [(i, i ^ (1 << apart)) for i in range(count)])


def leaf_kernel(first, moved, bases, out, held, arrived):
    count = out.shape[0]
    copies = []
    for i in range(count):
        copy = pltpu.make_async_copy(moved.at[pl.ds((first + i) * LEAF, LEAF)], held.at[i], arrived.at[i])
        copy.start()
        copies.append(copy)
    for i in range(count):
        copies[i].wait()
        out[i] = jnp.dot(bases[first + i], held[i], preferred_element_type=jnp.float32).astype(jnp.bfloat16)


def mixed(maps, state, other):
    values = jnp.concatenate([state, other], axis=0)
    return jnp.dot(maps, values, preferred_element_type=jnp.float32).astype(jnp.bfloat16)


def level_kernel(level, first, maps, state, other, out):
    for i in range(state.shape[0]):
        out[i] = mixed(maps[level - 1, first + i], state[i], other[i])


def last_kernel(level, first, maps, state, other, expand, *rest):
    out, held, sent = rest[-3:]
    copies = []
    for i in range(state.shape[0]):
        g = first + i
        final = mixed(maps[level - 1, g], state[i], other[i])
        rows = expand[pl.ds(g * LEAF, LEAF), :]
        held[i] = jnp.dot(rows, final, preferred_element_type=jnp.float32).astype(jnp.bfloat16)
        copy = pltpu.make_async_copy(held.at[i], out.at[pl.ds(g * LEAF, LEAF)], sent.at[i])
        copy.start()
        copies.append(copy)
    for copy in copies:
        copy.wait()


def limit(mib):
    return pltpu.CompilerParams(vmem_limit_bytes=mib * 1024 * 1024)


def cost(flops, size):
    return pl.CostEstimate(flops=flops, bytes_accessed=size, transcendentals=0)


def project(moved, bases, first, count):
    rhs, rank_max = moved.shape[1], bases.shape[1]
    return pl.pallas_call(
        functools.partial(leaf_kernel, first),
        out_shape=jax.ShapeDtypeStruct((count, rank_max, rhs), jnp.bfloat16),
        in_specs=[ANY, VMEM],
        out_specs=VMEM,
        scratch_shapes=[pltpu.VMEM((count, LEAF, rhs), jnp.bfloat16), pltpu.SemaphoreType.DMA((count,))],
        compiler_params=limit(24),
        cost_estimate=cost(2 * count * LEAF * rank_max * rhs, count * LEAF * rhs * 2),
        name="leaf",
    )(moved, bases)


def advance(state, other, maps, level, first):
    count, rank_max, rhs = state.shape
    return pl.pallas_call(
        functools.partial(level_kernel, level, first),
        out_shape=jax.ShapeDtypeStruct(state.shape, jnp.bfloat16),
        in_specs=[VMEM] * 3,
        out_specs=VMEM,
        compiler_params=limit(24),
        cost_estimate=cost(4 * count * rank_max * rank_max * rhs, count * rank_max * rhs * 2),
        name="level",
    )(maps, state, other)


def finish(state, other, maps, expand, level, first, so_far):
    count, rank_max, rhs = state.shape
    args = [maps, state, other, expand]
    specs = [VMEM] * 4
    alias = {}
    if so_far is not None:
        alias = {len(args): 0}
        args.append(so_far)
        specs.append(ANY)
    return pl.pallas_call(
        functools.partial(last_kernel, level, first),
        out_shape=jax.ShapeDtypeStruct((expand.shape[0], rhs), jnp.bfloat16),
        in_specs=specs,
        out_specs=ANY,
        scratch_shapes=[pltpu.VMEM((count, LEAF, rhs), jnp.bfloat16), pltpu.SemaphoreType.DMA((count,))],
        input_output_aliases=alias,
        compiler_params=limit(24),
        cost_estimate=cost(2 * count * rank_max * rhs * (LEAF + 2 * rank_max), count * LEAF * rhs * 2),
        name="finish",
    )(*args)


def on_device(points, leaf_bases, own_maps, partner_maps, expand_bases, ranks):
    moved = lax.all_to_all(points, ("row", "col"), split_axis=0, concat_axis=0, tiled=True)
    rank_max = leaf_bases.shape[1]
    keep = (jnp.arange(rank_max, dtype=jnp.int32) < ranks[:, :, None])[..., None]
    bases = jnp.where(keep[0], leaf_bases.reshape(-1, LEAF, rank_max).transpose(0, 2, 1), 0)
    maps = jnp.where(keep[1:], jnp.concatenate([own_maps, partner_maps], axis=3), 0)
    moved, bases, maps = lax.optimization_barrier((moved, bases, maps))
    col_bits = lax.axis_size("col").bit_length() - 1
    row_bits = lax.axis_size("row").bit_length() - 1
    pairs = [("col", col_bits - 1), ("col", col_bits - 2), ("col", col_bits - 3), ("row", row_bits - 1)]
    firsts = [sum(SIZES[:c]) for c in range(len(SIZES))]
    states = [project(moved, bases, f, n) for f, n in zip(firsts, SIZES)]
    for level in range(1, 4):
        others = [swapped(s, *pairs[level - 1]) for s in states]
        states = [advance(s, o, maps, level, f) for f, s, o in zip(firsts, states, others)]
    others = [swapped(s, *pairs[3]) for s in states]
    result = None
    for f, s, o in zip(firsts, states, others):
        result = finish(s, o, maps, expand_bases, 4, f, result)
    return result


def solution(mesh):
    return jax.shard_map(
        on_device,
        mesh=mesh,
        in_specs=(
            P(("row", "col"), None),
            P(("row", "col"), None),
            P(None, ("row", "col"), None, None),
            P(None, ("row", "col"), None, None),
            P(("row", "col"), None),
            P(None, ("row", "col")),
        ),
        out_specs=P(("row", "col"), None),
        check_vma=False,
    )
```

time: 181 us -> 137 us (0.76)
  waiting for transfers between devices: 146 us -> 85.5 us
  Pallas kernels: 0 us -> 16.6 us
  matrix products: 13.8 us -> 0 us
  starting transfers between devices: 13.6 us -> 24.8 us
  other arithmetic: 0.08 us -> 4.96 us
  local copies, waits for them, and re-layouts: 6.4 us -> 3.55 us
    ppermute x4 -> x16, waiting for transfers between devices: 95 us -> 42.5 us  [swapped(): lax.ppermute(block, axis, [(i, i ^ 1 << apart) for i in range(count)])]
    pallas_call x0 -> x20, Pallas kernels: none -> 16.6 us  [the longest x4 7.43 us: project(): pl.pallas_call(functools.partial(leaf_kernel, first), out_shape=jax.Shape...]
    dot_general x9 -> x0, matrix products: 13.8 us -> none  [the longest x1 5.25 us: on_device(): jnp.einsum('blk,bkr->blr', expand_bases.reshape(blocks, LEAF, rank_max),...]
    ppermute x4 -> x16, starting transfers between devices: 2.66 us -> 13.8 us  [swapped(): lax.ppermute(block, axis, [(i, i ^ 1 << apart) for i in range(count)])]
    all_to_all x1, waiting for transfers between devices: 51.4 us -> 43 us  [on_device(): lax.all_to_all(points, ('row', 'col'), split_axis=0, concat_axis=0, tiled...]
    convert_element_type x1 -> x0, local copies, waits for them, and re-layouts: 6.38 us -> none  [on_device(): return result.astype(jnp.bfloat16).reshape(p_dev, rhs)]
    select_n x0 -> x2, other arithmetic: none -> 4.88 us  [the longest x1 2.97 us: on_device(): jnp.where(keep[1:], jnp.concatenate([own_maps, partner_maps], axis=3), 0)]
    reshape x0 -> x1, local copies, waits for them, and re-layouts: none -> 2.6 us  [on_device(): leaf_bases.reshape(-1, LEAF, rank_max).transpose(0, 2, 1)]
  transfers between devices with their start and end apart: 5 -> 17, of which waited for: 5 -> 13; matrix products, arithmetic and copies ran while one was open for 2% -> 6% of each run, Pallas kernels for 0% -> 10%
where the time goes in v1:
time: 137 us; the launch traced here: 136 us
  waiting for transfers between devices  85.5 us (62%)
  starting transfers between devices  24.8 us (18%)
  Pallas kernels  16.6 us (12%)
  other arithmetic  4.96 us (4%)
  local copies, waits for them, and re-layouts  3.55 us (3%)
    all_to_all x1, waiting for transfers between devices, on_device(): lax.all_to_all(points, ('row', 'col'), split_axis=0, concat_axis=0, tiled...  43 us
    ppermute x16, waiting for transfers between devices, swapped(): lax.ppermute(block, axis, [(i, i ^ 1 << apart) for i in range(count)])  42.5 us
    ppermute x16, starting transfers between devices, swapped(): lax.ppermute(block, axis, [(i, i ^ 1 << apart) for i in range(count)])  13.8 us
    all_to_all x1, starting transfers between devices, on_device(): lax.all_to_all(points, ('row', 'col'), split_axis=0, concat_axis=0, tiled...  11 us
    pallas_call x4, Pallas kernels, project(): pl.pallas_call(functools.partial(leaf_kernel, first), out_shape=jax.Shape...  7.43 us
    pallas_call x4, Pallas kernels, finish(): pl.pallas_call(functools.partial(last_kernel, level, first), out_shape=ja...  6.4 us
    select_n x1, other arithmetic, on_device(): jnp.where(keep[1:], jnp.concatenate([own_maps, partner_maps], axis=3), 0)  2.97 us
    pallas_call x12, Pallas kernels, advance(): pl.pallas_call(functools.partial(level_kernel, level, first), out_shape=j...  2.79 us
  transfers between devices with their start and end apart: 17, of which 13 were waited for; matrix products, arithmetic and copies ran while one was open for 6% of the time, Pallas kernels for 10%

profile of v1, /device:TPU:2, one launch (start us, length us, event | category | flops | bytes accessed | tf_op | source)
XLA Modules:
  0.0 135.7 jit_solution(8355958440891094313)
XLA Ops:
  0.0 11.0 %all-to-all-start = ((bf16[128,64,256]{2,1,0:T(8,128)(2,1)}), bf16[128,64,256]{2,1,0:T(8,128)(2,1)}, u32[]{:S(2)}, u32[]{:S(2)}) async-start(bf16[128,64,256]{2,1,0:T(8,128)(2,1)} %bitcast.7), calls=%async_computation | async-start | bytes 8388608 | tf_op jit(solution)/shard_map/all_to_all | solution.py:116
  11.1 2.6 %copy.10 = bf16[16,512,128]{1,2,0:T(8,128)(2,1)} copy(bf16[16,512,128]{2,1,0:T(8,128)(2,1)S(1)} %bitcast.8) | data formatting | bytes 4194304 | tf_op jit(solution)/shard_map/reshape | solution.py:119
  13.7 1.9 %select_bitcast_fusion.bases = bf16[16,128,512]{2,1,0:T(8,128)(2,1)S(1)} fusion(bf16[16,512,128]{1,2,0:T(8,128)(2,1)} %copy.10, pred[16,128]{1,0:T(8,128)(4,1)S(1)} %slice_bitcast_fusion), kind=kLoop, calls=%fused_computation.1 | loop fusion | flops 1048576 | bytes 4196352 | tf_op jit(solution)/shard_map/jit(_where)/select_n | solution.py:119
  15.6 0.3 copy-done.2
  15.9 0.6 copy-done.3
  16.6 3.0 %maximum_select_fusion.maps = bf16[4,16,128,256]{3,2,1,0:T(8,128)(2,1)} fusion(bf16[4,16,128,128]{3,2,1,0:T(8,128)(2,1)S(1)} %copy-done.2, bf16[4,16,128,128]{3,2,1,0:T(8,128)(2,1)S(1)} %copy-done.3, pred[4,16,128]{2,1,0:T(8,128)(4,1)S(1)} %slice.11), kind=kLoop, calls=%fused_computation | loop fusion | flops 10485760 | bytes 8396800 | tf_op jit(solution)/shard_map/jit(_where)/select_n | solution.py:120
  19.5 43.0 %all-to-all-done = bf16[128,64,256]{2,1,0:T(8,128)(2,1)} async-done(((bf16[128,64,256]{2,1,0:T(8,128)(2,1)}), bf16[128,64,256]{2,1,0:T(8,128)(2,1)}, u32[]{:S(2)}, u32[]{:S(2)}) %all-to-all-start) | async-done | bytes 4194336 | tf_op jit(solution)/shard_map/all_to_all | solution.py:116
  62.5 1.9 %leaf.7.state = bf16[4,128,256]{2,1,0:T(8,128)(2,1)S(1)} custom-call(bf16[8192,256]{1,0:T(8,128)(2,1)} %bitcast.1.moved, bf16[16,128,512]{2,1,0:T(8,128)(2,1)S(1)} %select_bitcast_fusion.bases), custom_call_target="tpu_custom_call" | custom-call | flops 134217728 | bytes 1048576 | tf_op jit(solution)/shard_map/leaf/pallas_call | solution.py:68
  64.4 2.0 %collective-permute-start.12 = (bf16[4,128,256]{2,1,0:T(8,128)(2,1)S(1)}, bf16[4,128,256]{2,1,0:T(8,128)(2,1)S(1)}, u32[]{:S(2)}, u32[]{:S(2)}) collective-permute-start(bf16[4,128,256]{2,1,0:T(8,128)(2,1)S(1)} %leaf.7.state), channel_id=1, source_target_pairs={{0,8},{1,9},{2,10},{3,11},{4,12},{5,13},{6,14},{7,15},{8,0},{9,1},... | collective-permute-start | bytes 786440 | tf_op jit(solution)/shard_map/ppermute | solution.py:18
  66.3 1.9 %leaf.6.state = bf16[4,128,256]{2,1,0:T(8,128)(2,1)S(1)} custom-call(bf16[8192,256]{1,0:T(8,128)(2,1)} %bitcast.1.moved, bf16[16,128,512]{2,1,0:T(8,128)(2,1)S(1)} %select_bitcast_fusion.bases), custom_call_target="tpu_custom_call" | custom-call | flops 134217728 | bytes 1048576 | tf_op jit(solution)/shard_map/leaf/pallas_call | solution.py:68
  68.2 1.7 %collective-permute-start.8 = (bf16[4,128,256]{2,1,0:T(8,128)(2,1)S(1)}, bf16[4,128,256]{2,1,0:T(8,128)(2,1)S(1)}, u32[]{:S(2)}, u32[]{:S(2)}) collective-permute-start(bf16[4,128,256]{2,1,0:T(8,128)(2,1)S(1)} %leaf.6.state), channel_id=1, source_target_pairs={{0,8},{1,9},{2,10},{3,11},{4,12},{5,13},{6,14},{7,15},{8,0},{9,1},... | collective-permute-start | bytes 786440 | tf_op jit(solution)/shard_map/ppermute | solution.py:18
  69.9 1.9 %leaf.5.state = bf16[4,128,256]{2,1,0:T(8,128)(2,1)S(1)} custom-call(bf16[8192,256]{1,0:T(8,128)(2,1)} %bitcast.1.moved, bf16[16,128,512]{2,1,0:T(8,128)(2,1)S(1)} %select_bitcast_fusion.bases), custom_call_target="tpu_custom_call" | custom-call | flops 134217728 | bytes 1048576 | tf_op jit(solution)/shard_map/leaf/pallas_call | solution.py:68
  71.8 2.0 %collective-permute-start.4 = (bf16[4,128,256]{2,1,0:T(8,128)(2,1)S(1)}, bf16[4,128,256]{2,1,0:T(8,128)(2,1)S(1)}, u32[]{:S(2)}, u32[]{:S(2)}) collective-permute-start(bf16[4,128,256]{2,1,0:T(8,128)(2,1)S(1)} %leaf.5.state), channel_id=1, source_target_pairs={{0,8},{1,9},{2,10},{3,11},{4,12},{5,13},{6,14},{7,15},{8,0},{9,1},... | collective-permute-start | bytes 786440 | tf_op jit(solution)/shard_map/ppermute | solution.py:18
  73.8 1.9 %leaf.4.state = bf16[4,128,256]{2,1,0:T(8,128)(2,1)S(1)} custom-call(bf16[8192,256]{1,0:T(8,128)(2,1)} %bitcast.1.moved, bf16[16,128,512]{2,1,0:T(8,128)(2,1)S(1)} %select_bitcast_fusion.bases), custom_call_target="tpu_custom_call" | custom-call | flops 134217728 | bytes 1048576 | tf_op jit(solution)/shard_map/leaf/pallas_call | solution.py:68
  75.6 1.7 %collective-permute-start = (bf16[4,128,256]{2,1,0:T(8,128)(2,1)S(1)}, bf16[4,128,256]{2,1,0:T(8,128)(2,1)S(1)}, u32[]{:S(2)}, u32[]{:S(2)}) collective-permute-start(bf16[4,128,256]{2,1,0:T(8,128)(2,1)S(1)} %leaf.4.state), channel_id=1, source_target_pairs={{0,8},{1,9},{2,10},{3,11},{4,12},{5,13},{6,14},{7,15},{8,0},{9,1},... | collective-permute-start | bytes 786440 | tf_op jit(solution)/shard_map/ppermute | solution.py:18
  77.4 0.2 level.21.state
  77.6 0.7 collective-permute-start.13
  78.3 2.4 %collective-permute-done.8.other = bf16[4,128,256]{2,1,0:T(8,128)(2,1)S(1)} collective-permute-done((bf16[4,128,256]{2,1,0:T(8,128)(2,1)S(1)}, bf16[4,128,256]{2,1,0:T(8,128)(2,1)S(1)}, u32[]{:S(2)}, u32[]{:S(2)}) %collective-permute-start.8) | collective-permute-done | bytes 262176 | tf_op jit(solution)/shard_map/ppermute | solution.py:18
  80.9 0.6 collective-permute-start.9
  81.5 4.8 %collective-permute-done.4.other = bf16[4,128,256]{2,1,0:T(8,128)(2,1)S(1)} collective-permute-done((bf16[4,128,256]{2,1,0:T(8,128)(2,1)S(1)}, bf16[4,128,256]{2,1,0:T(8,128)(2,1)S(1)}, u32[]{:S(2)}, u32[]{:S(2)}) %collective-permute-start.4) | collective-permute-done | bytes 262176 | tf_op jit(solution)/shard_map/ppermute | solution.py:18
  86.3 0.2 level.15.state
  86.6 0.3 collective-permute-start.5
  86.9 4.4 %collective-permute-done.other = bf16[4,128,256]{2,1,0:T(8,128)(2,1)S(1)} collective-permute-done((bf16[4,128,256]{2,1,0:T(8,128)(2,1)S(1)}, bf16[4,128,256]{2,1,0:T(8,128)(2,1)S(1)}, u32[]{:S(2)}, u32[]{:S(2)}) %collective-permute-start) | collective-permute-done | bytes 262176 | tf_op jit(solution)/shard_map/ppermute | solution.py:18
  91.6 0.2 level.22.state
  91.8 1.6 %collective-permute-start.14 = (bf16[4,128,256]{2,1,0:T(8,128)(2,1)S(1)}, bf16[4,128,256]{2,1,0:T(8,128)(2,1)S(1)}, u32[]{:S(2)}, u32[]{:S(2)}) collective-permute-start(bf16[4,128,256]{2,1,0:T(8,128)(2,1)S(1)} %level.22.state), channel_id=1, source_target_pairs={{0,2},{1,3},{2,0},{3,1},{4,6},{5,7},{6,4},{7,5},{8,10},{9,11},{10,... | collective-permute-start | bytes 786440 | tf_op jit(solution)/shard_map/ppermute | solution.py:18
  93.4 0.6 collective-permute-done.9.other
  94.0 0.2 level.19.state
  94.3 0.4 collective-permute-start.10
  94.7 5.0 %collective-permute-done.5.other = bf16[4,128,256]{2,1,0:T(8,128)(2,1)S(1)} collective-permute-done((bf16[4,128,256]{2,1,0:T(8,128)(2,1)S(1)}, bf16[4,128,256]{2,1,0:T(8,128)(2,1)S(1)}, u32[]{:S(2)}, u32[]{:S(2)}) %collective-permute-start.5) | collective-permute-done | bytes 262176 | tf_op jit(solution)/shard_map/ppermute | solution.py:18
  99.9 0.4 collective-permute-start.6
  100.3 5.0 %collective-permute-done.1.other = bf16[4,128,256]{2,1,0:T(8,128)(2,1)S(1)} collective-permute-done((bf16[4,128,256]{2,1,0:T(8,128)(2,1)S(1)}, bf16[4,128,256]{2,1,0:T(8,128)(2,1)S(1)}, u32[]{:S(2)}, u32[]{:S(2)}) %collective-permute-start.1) | collective-permute-done | bytes 262176 | tf_op jit(solution)/shard_map/ppermute | solution.py:18
  105.5 0.4 collective-permute-start.2
  105.9 3.1 %collective-permute-done.14.other = bf16[4,128,256]{2,1,0:T(8,128)(2,1)S(1)} collective-permute-done((bf16[4,128,256]{2,1,0:T(8,128)(2,1)S(1)}, bf16[4,128,256]{2,1,0:T(8,128)(2,1)S(1)}, u32[]{:S(2)}, u32[]{:S(2)}) %collective-permute-start.14) | collective-permute-done | bytes 262176 | tf_op jit(solution)/shard_map/ppermute | solution.py:18
  109.2 0.5 collective-permute-start.15
  109.7 4.9 %collective-permute-done.10.other = bf16[4,128,256]{2,1,0:T(8,128)(2,1)S(1)} collective-permute-done((bf16[4,128,256]{2,1,0:T(8,128)(2,1)S(1)}, bf16[4,128,256]{2,1,0:T(8,128)(2,1)S(1)}, u32[]{:S(2)}, u32[]{:S(2)}) %collective-permute-start.10) | collective-permute-done | bytes 262176 | tf_op jit(solution)/shard_map/ppermute | solution.py:18
  114.6 0.2 level.20.state
  114.9 0.5 collective-permute-start.11
  115.3 4.9 %collective-permute-done.6.other = bf16[4,128,256]{2,1,0:T(8,128)(2,1)S(1)} collective-permute-done((bf16[4,128,256]{2,1,0:T(8,128)(2,1)S(1)}, bf16[4,128,256]{2,1,0:T(8,128)(2,1)S(1)}, u32[]{:S(2)}, u32[]{:S(2)}) %collective-permute-start.6) | collective-permute-done | bytes 262176 | tf_op jit(solution)/shard_map/ppermute | solution.py:18
  120.5 0.5 collective-permute-start.7
  121.0 3.1 %collective-permute-done.2.other = bf16[4,128,256]{2,1,0:T(8,128)(2,1)S(1)} collective-permute-done((bf16[4,128,256]{2,1,0:T(8,128)(2,1)S(1)}, bf16[4,128,256]{2,1,0:T(8,128)(2,1)S(1)}, u32[]{:S(2)}, u32[]{:S(2)}) %collective-permute-start.2) | collective-permute-done | bytes 262176 | tf_op jit(solution)/shard_map/ppermute | solution.py:18
  124.1 0.2 level.14.state
  124.3 0.5 collective-permute-start.3
  124.9 1.6 %finish.4.rest_0_ = bf16[8192,256]{1,0:T(8,128)(2,1)} custom-call(bf16[4,16,128,256]{3,2,1,0:T(8,128)(2,1)S(1)} %copy-done, bf16[4,128,256]{2,1,0:T(8,128)(2,1)S(1)} %level.23.state, bf16[4,128,256]{2,1,0:T(8,128)(2,1)S(1)} %collective-permute-done.15.other, bf16[8192,128]{1,0:T(8,128)(2,1)S(1)} %copy-done.1), custom_call_target="tpu_custom_call" | custom-call | flops 201326592 | bytes 1048576 | tf_op jit(solution)/shard_map/finish/pallas_call | solution.py:102
  126.5 1.6 %finish.5.rest_0_ = bf16[8192,256]{1,0:T(8,128)(2,1)} custom-call(bf16[4,16,128,256]{3,2,1,0:T(8,128)(2,1)S(1)} %copy-done, bf16[4,128,256]{2,1,0:T(8,128)(2,1)S(1)} %level.20.state, bf16[4,128,256]{2,1,0:T(8,128)(2,1)S(1)} %collective-permute-done.11.other, bf16[8192,128]{1,0:T(8,128)(2,1)S(1)} %copy-done.1, ...), custom_call_target="tpu_custom_call", output_to_operand_aliasing={{}: (4, {})} | custom-call | flops 201326592 | bytes 1048576 | tf_op jit(solution)/shard_map/finish/pallas_call | solution.py:102
  128.1 1.9 %collective-permute-done.7.other = bf16[4,128,256]{2,1,0:T(8,128)(2,1)S(1)} collective-permute-done((bf16[4,128,256]{2,1,0:T(8,128)(2,1)S(1)}, bf16[4,128,256]{2,1,0:T(8,128)(2,1)S(1)}, u32[]{:S(2)}, u32[]{:S(2)}) %collective-permute-start.7) | collective-permute-done | bytes 262176 | tf_op jit(solution)/shard_map/ppermute | solution.py:18
  130.0 1.6 %finish.6.rest_0_ = bf16[8192,256]{1,0:T(8,128)(2,1)} custom-call(bf16[4,16,128,256]{3,2,1,0:T(8,128)(2,1)S(1)} %copy-done, bf16[4,128,256]{2,1,0:T(8,128)(2,1)S(1)} %level.17.state, bf16[4,128,256]{2,1,0:T(8,128)(2,1)S(1)} %collective-permute-done.7.other, bf16[8192,128]{1,0:T(8,128)(2,1)S(1)} %copy-done.1, ...), custom_call_target="tpu_custom_call", output_to_operand_aliasing={{}: (4, {})} | custom-call | flops 201326592 | bytes 1048576 | tf_op jit(solution)/shard_map/finish/pallas_call | solution.py:102
  131.6 2.5 %collective-permute-done.3.other = bf16[4,128,256]{2,1,0:T(8,128)(2,1)S(1)} collective-permute-done((bf16[4,128,256]{2,1,0:T(8,128)(2,1)S(1)}, bf16[4,128,256]{2,1,0:T(8,128)(2,1)S(1)}, u32[]{:S(2)}, u32[]{:S(2)}) %collective-permute-start.3) | collective-permute-done | bytes 262176 | tf_op jit(solution)/shard_map/ppermute | solution.py:18
  134.1 1.6 %finish.7 = bf16[8192,256]{1,0:T(8,128)(2,1)} custom-call(bf16[4,16,128,256]{3,2,1,0:T(8,128)(2,1)S(1)} %copy-done, bf16[4,128,256]{2,1,0:T(8,128)(2,1)S(1)} %level.14.state, bf16[4,128,256]{2,1,0:T(8,128)(2,1)S(1)} %collective-permute-done.3.other, bf16[8192,128]{1,0:T(8,128)(2,1)S(1)} %copy-done.1, ...), custom_call_target="tpu_custom_call", output_to_operand_aliasing={{}: (4, {})} | custom-call | flops 201326592 | bytes 1048576 | tf_op jit(solution)/shard_map/finish/pallas_call | solution.py:102
  (24 shorter events, 1.6 us)
Async XLA Ops:
  0.0 11.0 %copy-start.5 = (s32[5,16]{1,0:T(8,128)S(1)}, s32[5,16]{1,0:T(8,128)}, u32[]{:S(2)}) copy-start(s32[5,16]{1,0:T(8,128)} %param.11) | copy-start | bytes 964
  0.0 11.1 %copy-start.4 = (bf16[8192,128]{1,0:T(8,128)(2,1)S(1)}, bf16[8192,128]{1,0:T(8,128)(2,1)}, u32[]{:S(2)}) copy-start(bf16[8192,128]{1,0:T(8,128)(2,1)} %param.7) | copy-start | bytes 6291460
  0.0 62.5 %all-to-all-start = ((bf16[128,64,256]{2,1,0:T(8,128)(2,1)}), bf16[128,64,256]{2,1,0:T(8,128)(2,1)}, u32[]{:S(2)}, u32[]{:S(2)}) async-start(bf16[128,64,256]{2,1,0:T(8,128)(2,1)} %bitcast.7), calls=%async_computation | async-start | bytes 8388608 | tf_op jit(solution)/shard_map/all_to_all | solution.py:116
  13.7 2.2 %copy-start.2 = (bf16[4,16,128,128]{3,2,1,0:T(8,128)(2,1)S(1)}, bf16[4,16,128,128]{3,2,1,0:T(8,128)(2,1)}, u32[]{:S(2)}) copy-start(bf16[4,16,128,128]{3,2,1,0:T(8,128)(2,1)} %param.9) | copy-start | bytes 6291460
  13.7 2.9 %copy-start.3 = (bf16[4,16,128,128]{3,2,1,0:T(8,128)(2,1)S(1)}, bf16[4,16,128,128]{3,2,1,0:T(8,128)(2,1)}, u32[]{:S(2)}) copy-start(bf16[4,16,128,128]{3,2,1,0:T(8,128)(2,1)} %param.8) | copy-start | bytes 6291460
  64.4 13.0 %collective-permute-start.12 = (bf16[4,128,256]{2,1,0:T(8,128)(2,1)S(1)}, bf16[4,128,256]{2,1,0:T(8,128)(2,1)S(1)}, u32[]{:S(2)}, u32[]{:S(2)}) collective-permute-start(bf16[4,128,256]{2,1,0:T(8,128)(2,1)S(1)} %leaf.7.state), channel_id=1, source_target_pairs={{0,8},{1,9},{2,10},{3,11},{4,12},{5,13},{6,14},{7,15},{8,0},{9,1},... | collective-permute-start | bytes 786440 | tf_op jit(solution)/shard_map/ppermute | solution.py:18
  68.2 12.5 %collective-permute-start.8 = (bf16[4,128,256]{2,1,0:T(8,128)(2,1)S(1)}, bf16[4,128,256]{2,1,0:T(8,128)(2,1)S(1)}, u32[]{:S(2)}, u32[]{:S(2)}) collective-permute-start(bf16[4,128,256]{2,1,0:T(8,128)(2,1)S(1)} %leaf.6.state), channel_id=1, source_target_pairs={{0,8},{1,9},{2,10},{3,11},{4,12},{5,13},{6,14},{7,15},{8,0},{9,1},... | collective-permute-start | bytes 786440 | tf_op jit(solution)/shard_map/ppermute | solution.py:18
  71.8 5.6 %copy-start = (bf16[4,16,128,256]{3,2,1,0:T(8,128)(2,1)S(1)}, bf16[4,16,128,256]{3,2,1,0:T(8,128)(2,1)}, u32[]{:S(2)}) copy-start(bf16[4,16,128,256]{3,2,1,0:T(8,128)(2,1)} %maximum_select_fusion.maps) | copy-start | bytes 12582916
  71.8 14.5 %collective-permute-start.4 = (bf16[4,128,256]{2,1,0:T(8,128)(2,1)S(1)}, bf16[4,128,256]{2,1,0:T(8,128)(2,1)S(1)}, u32[]{:S(2)}, u32[]{:S(2)}) collective-permute-start(bf16[4,128,256]{2,1,0:T(8,128)(2,1)S(1)} %leaf.5.state), channel_id=1, source_target_pairs={{0,8},{1,9},{2,10},{3,11},{4,12},{5,13},{6,14},{7,15},{8,0},{9,1},... | collective-permute-start | bytes 786440 | tf_op jit(solution)/shard_map/ppermute | solution.py:18
  75.6 15.6 %collective-permute-start = (bf16[4,128,256]{2,1,0:T(8,128)(2,1)S(1)}, bf16[4,128,256]{2,1,0:T(8,128)(2,1)S(1)}, u32[]{:S(2)}, u32[]{:S(2)}) collective-permute-start(bf16[4,128,256]{2,1,0:T(8,128)(2,1)S(1)} %leaf.4.state), channel_id=1, source_target_pairs={{0,8},{1,9},{2,10},{3,11},{4,12},{5,13},{6,14},{7,15},{8,0},{9,1},... | collective-permute-start | bytes 786440 | tf_op jit(solution)/shard_map/ppermute | solution.py:18
  77.6 14.0 %collective-permute-start.13 = (bf16[4,128,256]{2,1,0:T(8,128)(2,1)S(1)}, bf16[4,128,256]{2,1,0:T(8,128)(2,1)S(1)}, u32[]{:S(2)}, u32[]{:S(2)}) collective-permute-start(bf16[4,128,256]{2,1,0:T(8,128)(2,1)S(1)} %level.21.state), channel_id=1, source_target_pairs={{0,4},{1,5},{2,6},{3,7},{4,0},{5,1},{6,2},{7,3},{8,12},{9,13},{10,... | collective-permute-start | bytes 786440 | tf_op jit(solution)/shard_map/ppermute | solution.py:18
  80.9 13.1 %collective-permute-start.9 = (bf16[4,128,256]{2,1,0:T(8,128)(2,1)S(1)}, bf16[4,128,256]{2,1,0:T(8,128)(2,1)S(1)}, u32[]{:S(2)}, u32[]{:S(2)}) collective-permute-start(bf16[4,128,256]{2,1,0:T(8,128)(2,1)S(1)} %level.18.state), channel_id=1, source_target_pairs={{0,4},{1,5},{2,6},{3,7},{4,0},{5,1},{6,2},{7,3},{8,12},{9,13},{10,... | collective-permute-start | bytes 786440 | tf_op jit(solution)/shard_map/ppermute | solution.py:18
  86.6 13.1 %collective-permute-start.5 = (bf16[4,128,256]{2,1,0:T(8,128)(2,1)S(1)}, bf16[4,128,256]{2,1,0:T(8,128)(2,1)S(1)}, u32[]{:S(2)}, u32[]{:S(2)}) collective-permute-start(bf16[4,128,256]{2,1,0:T(8,128)(2,1)S(1)} %level.15.state), channel_id=1, source_target_pairs={{0,4},{1,5},{2,6},{3,7},{4,0},{5,1},{6,2},{7,3},{8,12},{9,13},{10,... | collective-permute-start | bytes 786440 | tf_op jit(solution)/shard_map/ppermute | solution.py:18
  91.5 13.8 %collective-permute-start.1 = (bf16[4,128,256]{2,1,0:T(8,128)(2,1)S(1)}, bf16[4,128,256]{2,1,0:T(8,128)(2,1)S(1)}, u32[]{:S(2)}, u32[]{:S(2)}) collective-permute-start(bf16[4,128,256]{2,1,0:T(8,128)(2,1)S(1)} %level.12.state), channel_id=1, source_target_pairs={{0,4},{1,5},{2,6},{3,7},{4,0},{5,1},{6,2},{7,3},{8,12},{9,13},{10,... | collective-permute-start | bytes 786440 | tf_op jit(solution)/shard_map/ppermute | solution.py:18
  91.8 17.2 %collective-permute-start.14 = (bf16[4,128,256]{2,1,0:T(8,128)(2,1)S(1)}, bf16[4,128,256]{2,1,0:T(8,128)(2,1)S(1)}, u32[]{:S(2)}, u32[]{:S(2)}) collective-permute-start(bf16[4,128,256]{2,1,0:T(8,128)(2,1)S(1)} %level.22.state), channel_id=1, source_target_pairs={{0,2},{1,3},{2,0},{3,1},{4,6},{5,7},{6,4},{7,5},{8,10},{9,11},{10,... | collective-permute-start | bytes 786440 | tf_op jit(solution)/shard_map/ppermute | solution.py:18
  94.3 20.3 %collective-permute-start.10 = (bf16[4,128,256]{2,1,0:T(8,128)(2,1)S(1)}, bf16[4,128,256]{2,1,0:T(8,128)(2,1)S(1)}, u32[]{:S(2)}, u32[]{:S(2)}) collective-permute-start(bf16[4,128,256]{2,1,0:T(8,128)(2,1)S(1)} %level.19.state), channel_id=1, source_target_pairs={{0,2},{1,3},{2,0},{3,1},{4,6},{5,7},{6,4},{7,5},{8,10},{9,11},{10,... | collective-permute-start | bytes 786440 | tf_op jit(solution)/shard_map/ppermute | solution.py:18
  99.9 20.3 %collective-permute-start.6 = (bf16[4,128,256]{2,1,0:T(8,128)(2,1)S(1)}, bf16[4,128,256]{2,1,0:T(8,128)(2,1)S(1)}, u32[]{:S(2)}, u32[]{:S(2)}) collective-permute-start(bf16[4,128,256]{2,1,0:T(8,128)(2,1)S(1)} %level.16.state), channel_id=1, source_target_pairs={{0,2},{1,3},{2,0},{3,1},{4,6},{5,7},{6,4},{7,5},{8,10},{9,11},{10,... | collective-permute-start | bytes 786440 | tf_op jit(solution)/shard_map/ppermute | solution.py:18
  105.5 18.6 %collective-permute-start.2 = (bf16[4,128,256]{2,1,0:T(8,128)(2,1)S(1)}, bf16[4,128,256]{2,1,0:T(8,128)(2,1)S(1)}, u32[]{:S(2)}, u32[]{:S(2)}) collective-permute-start(bf16[4,128,256]{2,1,0:T(8,128)(2,1)S(1)} %level.13.state), channel_id=1, source_target_pairs={{0,2},{1,3},{2,0},{3,1},{4,6},{5,7},{6,4},{7,5},{8,10},{9,11},{10,... | collective-permute-start | bytes 786440 | tf_op jit(solution)/shard_map/ppermute | solution.py:18
  109.2 15.6 %collective-permute-start.15 = (bf16[4,128,256]{2,1,0:T(8,128)(2,1)S(1)}, bf16[4,128,256]{2,1,0:T(8,128)(2,1)S(1)}, u32[]{:S(2)}, u32[]{:S(2)}) collective-permute-start(bf16[4,128,256]{2,1,0:T(8,128)(2,1)S(1)} %level.23.state), channel_id=1, source_target_pairs={{0,64},{16,80},{32,96},{48,112},{64,0},{80,16},{96,32},{112,48},{1... | collective-permute-start | bytes 786440 | tf_op jit(solution)/shard_map/ppermute | solution.py:18
  114.9 10.0 %copy-start.1 = (bf16[8192,128]{1,0:T(8,128)(2,1)S(1)}, bf16[8192,128]{1,0:T(8,128)(2,1)}, u32[]{:S(2)}) copy-start(bf16[8192,128]{1,0:T(8,128)(2,1)} %expand.7) | copy-start | bytes 6291460
  114.9 11.6 %collective-permute-start.11 = (bf16[4,128,256]{2,1,0:T(8,128)(2,1)S(1)}, bf16[4,128,256]{2,1,0:T(8,128)(2,1)S(1)}, u32[]{:S(2)}, u32[]{:S(2)}) collective-permute-start(bf16[4,128,256]{2,1,0:T(8,128)(2,1)S(1)} %level.20.state), channel_id=1, source_target_pairs={{0,64},{16,80},{32,96},{48,112},{64,0},{80,16},{96,32},{112,48},{1... | collective-permute-start | bytes 786440 | tf_op jit(solution)/shard_map/ppermute | solution.py:18
  120.5 9.5 %collective-permute-start.7 = (bf16[4,128,256]{2,1,0:T(8,128)(2,1)S(1)}, bf16[4,128,256]{2,1,0:T(8,128)(2,1)S(1)}, u32[]{:S(2)}, u32[]{:S(2)}) collective-permute-start(bf16[4,128,256]{2,1,0:T(8,128)(2,1)S(1)} %level.17.state), channel_id=1, source_target_pairs={{0,64},{16,80},{32,96},{48,112},{64,0},{80,16},{96,32},{112,48},{1... | collective-permute-start | bytes 786440 | tf_op jit(solution)/shard_map/ppermute | solution.py:18
  124.3 9.7 %collective-permute-start.3 = (bf16[4,128,256]{2,1,0:T(8,128)(2,1)S(1)}, bf16[4,128,256]{2,1,0:T(8,128)(2,1)S(1)}, u32[]{:S(2)}, u32[]{:S(2)}) collective-permute-start(bf16[4,128,256]{2,1,0:T(8,128)(2,1)S(1)} %level.14.state), channel_id=1, source_target_pairs={{0,64},{16,80},{32,96},{48,112},{64,0},{80,16},{96,32},{112,48},{1... | collective-permute-start | bytes 786440 | tf_op jit(solution)/shard_map/ppermute | solution.py:18

commit v2 on v1

v2 whole, which is shorter than its diff:
```python
import functools

import jax
import jax.numpy as jnp
from jax import lax
from jax.experimental import pallas as pl
from jax.experimental.pallas import tpu as pltpu
from jax.sharding import PartitionSpec as P

LEAF = 512
GROUPS = [[4], [4, 4, 4]]
SIZES = sum(GROUPS, [])
VMEM = pl.BlockSpec(memory_space=pltpu.VMEM)
ANY = pl.BlockSpec(memory_space=pl.ANY)


def swapped(block, axis, apart):
    count = lax.axis_size(axis)
    return lax.ppermute(block, axis, [(i, i ^ (1 << apart)) for i in range(count)])


def leaf_kernel(first, outs, moved, bases, *rest):
    held, arrived = rest[-2:]
    places = [(out, i) for out in rest[-2 - outs : -2] for i in range(out.shape[0])]
    copies = []
    for n in range(len(places)):
        copy = pltpu.make_async_copy(moved.at[pl.ds((first + n) * LEAF, LEAF)], held.at[n], arrived.at[n])
        copy.start()
        copies.append(copy)
    for n, (out, i) in enumerate(places):
        copies[n].wait()
        out[i] = jnp.dot(bases[first + n], held[n], preferred_element_type=jnp.float32).astype(jnp.bfloat16)


def mixed(maps, state, other):
    values = jnp.concatenate([state, other], axis=0)
    return jnp.dot(maps, values, preferred_element_type=jnp.float32).astype(jnp.bfloat16)


def level_kernel(level, first, maps, state, other, *rest):
    out = rest[-1]
    for i in range(state.shape[0]):
        out[i] = mixed(maps[level - 1, first + i], state[i], other[i])


def last_kernel(level, first, maps, state, other, expand, *rest):
    out, held, sent = rest[-3:]
    copies = []
    for i in range(state.shape[0]):
        g = first + i
        final = mixed(maps[level - 1, g], state[i], other[i])
        rows = expand[pl.ds(g * LEAF, LEAF), :]
        held[i] = jnp.dot(rows, final, preferred_element_type=jnp.float32).astype(jnp.bfloat16)
        copy = pltpu.make_async_copy(held.at[i], out.at[pl.ds(g * LEAF, LEAF)], sent.at[i])
        copy.start()
        copies.append(copy)
    for copy in copies:
        copy.wait()


def limit(mib):
    return pltpu.CompilerParams(vmem_limit_bytes=mib * 1024 * 1024)


def cost(flops, size):
    return pl.CostEstimate(flops=0, bytes_accessed=0, transcendentals=0)


def project(moved, bases, first, counts, after):
    rhs, rank_max = moved.shape[1], bases.shape[1]
    count = sum(counts)
    return pl.pallas_call(
        functools.partial(leaf_kernel, first, len(counts)),
        out_shape=[jax.ShapeDtypeStruct((n, rank_max, rhs), jnp.bfloat16) for n in counts],
        in_specs=[ANY, VMEM] + [ANY] * len(after),
        out_specs=[VMEM] * len(counts),
        scratch_shapes=[pltpu.VMEM((count, LEAF, rhs), jnp.bfloat16), pltpu.SemaphoreType.DMA((count,))],
        compiler_params=limit(24),
        cost_estimate=cost(2 * count * LEAF * rank_max * rhs, count * LEAF * rhs * 2),
        name="leaf",
    )(moved, bases, *after)


def advance(state, other, maps, level, first, after):
    count, rank_max, rhs = state.shape
    return pl.pallas_call(
        functools.partial(level_kernel, level, first),
        out_shape=jax.ShapeDtypeStruct(state.shape, jnp.bfloat16),
        in_specs=[VMEM] * 3 + [ANY] * len(after),
        out_specs=VMEM,
        compiler_params=limit(24),
        cost_estimate=cost(4 * count * rank_max * rank_max * rhs, count * rank_max * rhs * 2),
        name="level",
    )(maps, state, other, *after)


def finish(state, other, maps, expand, level, first, after):
    count, rank_max, rhs = state.shape
    return pl.pallas_call(
        functools.partial(last_kernel, level, first),
        out_shape=jax.ShapeDtypeStruct((expand.shape[0], rhs), jnp.bfloat16),
        in_specs=[VMEM] * 4 + [ANY] * len(after),
        out_specs=ANY,
        scratch_shapes=[pltpu.VMEM((count, LEAF, rhs), jnp.bfloat16), pltpu.SemaphoreType.DMA((count,))],
        input_output_aliases={4: 0} if first else {},
        compiler_params=limit(24),
        cost_estimate=cost(2 * count * rank_max * rhs * (LEAF + 2 * rank_max), count * LEAF * rhs * 2),
        name="finish",
    )(maps, state, other, expand, *after)


def on_device(points, leaf_bases, own_maps, partner_maps, expand_bases, ranks):
    moved = lax.all_to_all(points, ("row", "col"), split_axis=0, concat_axis=0, tiled=True)
    rank_max = leaf_bases.shape[1]
    keep = (jnp.arange(rank_max, dtype=jnp.int32) < ranks[:, :, None])[..., None]
    bases = jnp.where(keep[0], leaf_bases.reshape(-1, LEAF, rank_max).transpose(0, 2, 1), 0)
    maps = jnp.where(keep[1:], jnp.concatenate([own_maps, partner_maps], axis=3), 0)
    moved, bases, maps = lax.optimization_barrier((moved, bases, maps))
    col_bits = lax.axis_size("col").bit_length() - 1
    row_bits = lax.axis_size("row").bit_length() - 1
    pairs = [("col", col_bits - 1), ("col", col_bits - 2), ("col", col_bits - 3), ("row", row_bits - 1)]
    chunks, first = [], 0
    for count in SIZES:
        chunks.append((first, count))
        first += count
    states, last, first = [], [], 0
    for counts in GROUPS:
        states += project(moved, bases, first, counts, last)
        last = [states[-1]]
        first += sum(counts)
    for level in range(1, 4):
        others = [swapped(s, *pairs[level - 1]) for s in states]
        for c, (first, _) in enumerate(chunks):
            states[c] = advance(states[c], others[c], maps, level, first, last)
            last = [states[c]]
    others = [swapped(s, *pairs[3]) for s in states]
    last = []
    for (first, _), state, other in zip(chunks, states, others):
        last = [finish(state, other, maps, expand_bases, 4, first, last)]
    return last[0]


def solution(mesh):
    return jax.shard_map(
        on_device,
        mesh=mesh,
        in_specs=(
            P(("row", "col"), None),
            P(("row", "col"), None),
            P(None, ("row", "col"), None, None),
            P(None, ("row", "col"), None, None),
            P(("row", "col"), None),
            P(None, ("row", "col")),
        ),
        out_specs=P(("row", "col"), None),
        check_vma=False,
    )
```

time: 137 us -> 134 us (0.978)
  waiting for transfers between devices: 85.5 us -> 81.7 us
  starting transfers between devices: 24.8 us -> 28.3 us
  Pallas kernels: 16.6 us -> 14.7 us
    ppermute x16, waiting for transfers between devices: 42.5 us -> 38.7 us  [swapped(): lax.ppermute(block, axis, [(i, i ^ 1 << apart) for i in range(count)])]
    ppermute x16, starting transfers between devices: 13.8 us -> 17.3 us  [swapped(): lax.ppermute(block, axis, [(i, i ^ 1 << apart) for i in range(count)])]
    pallas_call x4 -> x2, Pallas kernels: 7.43 us -> 5.54 us  [project(): pl.pallas_call(functools.partial(leaf_kernel, first, len(counts)), out_sh...]
  transfers between devices with their start and end apart: 17 -> 17, of which waited for: 13 -> 12; matrix products, arithmetic and copies ran while one was open for 6% -> 6% of each run, Pallas kernels for 10% -> 8%
where the time goes in v2:
time: 134 us; the launch traced here: 133 us
  waiting for transfers between devices  81.7 us (61%)
  starting transfers between devices  28.3 us (21%)
  Pallas kernels  14.7 us (11%)
  other arithmetic  4.96 us (4%)
  local copies, waits for them, and re-layouts  3.55 us (3%)
    all_to_all x1, waiting for transfers between devices, on_device(): lax.all_to_all(points, ('row', 'col'), split_axis=0, concat_axis=0, tiled...  43 us
    ppermute x16, waiting for transfers between devices, swapped(): lax.ppermute(block, axis, [(i, i ^ 1 << apart) for i in range(count)])  38.7 us
    ppermute x16, starting transfers between devices, swapped(): lax.ppermute(block, axis, [(i, i ^ 1 << apart) for i in range(count)])  17.3 us
    all_to_all x1, starting transfers between devices, on_device(): lax.all_to_all(points, ('row', 'col'), split_axis=0, concat_axis=0, tiled...  11 us
    pallas_call x4, Pallas kernels, finish(): pl.pallas_call(functools.partial(last_kernel, level, first), out_shape=ja...  6.4 us
    pallas_call x2, Pallas kernels, project(): pl.pallas_call(functools.partial(leaf_kernel, first, len(counts)), out_sh...  5.54 us
    select_n x1, other arithmetic, on_device(): jnp.where(keep[1:], jnp.concatenate([own_maps, partner_maps], axis=3), 0)  2.97 us
    pallas_call x12, Pallas kernels, advance(): pl.pallas_call(functools.partial(level_kernel, level, first), out_shape=j...  2.79 us
  transfers between devices with their start and end apart: 17, of which 12 were waited for; matrix products, arithmetic and copies ran while one was open for 6% of the time, Pallas kernels for 8%

profile of v2, /device:TPU:2, one launch (start us, length us, event | category | flops | bytes accessed | tf_op | source)
XLA Modules:
  0.0 133.4 jit_solution(2201890256384147429)
XLA Ops:
  0.0 11.0 %all-to-all-start = ((bf16[128,64,256]{2,1,0:T(8,128)(2,1)}), bf16[128,64,256]{2,1,0:T(8,128)(2,1)}, u32[]{:S(2)}, u32[]{:S(2)}) async-start(bf16[128,64,256]{2,1,0:T(8,128)(2,1)} %bitcast.7), calls=%async_computation | async-start | bytes 8388608 | tf_op jit(solution)/shard_map/all_to_all | solution.py:113
  11.1 2.6 %copy.10 = bf16[16,512,128]{1,2,0:T(8,128)(2,1)} copy(bf16[16,512,128]{2,1,0:T(8,128)(2,1)S(1)} %bitcast.8) | data formatting | bytes 4194304 | tf_op jit(solution)/shard_map/reshape | solution.py:116
  13.7 1.9 %select_bitcast_fusion.bases = bf16[16,128,512]{2,1,0:T(8,128)(2,1)S(1)} fusion(bf16[16,512,128]{1,2,0:T(8,128)(2,1)} %copy.10, pred[16,128]{1,0:T(8,128)(4,1)S(1)} %slice_bitcast_fusion), kind=kLoop, calls=%fused_computation.1 | loop fusion | flops 1048576 | bytes 4196352 | tf_op jit(solution)/shard_map/jit(_where)/select_n | solution.py:116
  15.6 0.3 copy-done.2
  15.9 0.6 copy-done.3
  16.6 3.0 %maximum_select_fusion.maps = bf16[4,16,128,256]{3,2,1,0:T(8,128)(2,1)} fusion(bf16[4,16,128,128]{3,2,1,0:T(8,128)(2,1)S(1)} %copy-done.2, bf16[4,16,128,128]{3,2,1,0:T(8,128)(2,1)S(1)} %copy-done.3, pred[4,16,128]{2,1,0:T(8,128)(4,1)S(1)} %slice.11), kind=kLoop, calls=%fused_computation | loop fusion | flops 10485760 | bytes 8396800 | tf_op jit(solution)/shard_map/jit(_where)/select_n | solution.py:117
  19.5 43.0 %all-to-all-done = bf16[128,64,256]{2,1,0:T(8,128)(2,1)} async-done(((bf16[128,64,256]{2,1,0:T(8,128)(2,1)}), bf16[128,64,256]{2,1,0:T(8,128)(2,1)}, u32[]{:S(2)}, u32[]{:S(2)}) %all-to-all-start) | async-done | bytes 4194336 | tf_op jit(solution)/shard_map/all_to_all | solution.py:113
  62.5 1.9 %leaf.2.rest_0_.state = bf16[4,128,256]{2,1,0:T(8,128)(2,1)S(1)} custom-call(bf16[8192,256]{1,0:T(8,128)(2,1)} %bitcast.1.moved, bf16[16,128,512]{2,1,0:T(8,128)(2,1)S(1)} %select_bitcast_fusion.bases), custom_call_target="tpu_custom_call" | custom-call | tf_op jit(solution)/shard_map/leaf/pallas_call | solution.py:72
  64.4 2.0 %collective-permute-start.3 = (bf16[4,128,256]{2,1,0:T(8,128)(2,1)S(1)}, bf16[4,128,256]{2,1,0:T(8,128)(2,1)S(1)}, u32[]{:S(2)}, u32[]{:S(2)}) collective-permute-start(bf16[4,128,256]{2,1,0:T(8,128)(2,1)S(1)} %leaf.2.rest_0_.state), channel_id=1, source_target_pairs={{0,8},{1,9},{2,10},{3,11},{4,12},{5,13},{6,14},{7,15},{8,0},{9,1},... | collective-permute-start | bytes 786440 | tf_op jit(solution)/shard_map/ppermute | solution.py:19
  66.3 3.7 %leaf.3 = (bf16[4,128,256]{2,1,0:T(8,128)(2,1)S(1)}, bf16[4,128,256]{2,1,0:T(8,128)(2,1)S(1)}, bf16[4,128,256]{2,1,0:T(8,128)(2,1)S(1)}) custom-call(bf16[8192,256]{1,0:T(8,128)(2,1)} %bitcast.1.moved, bf16[16,128,512]{2,1,0:T(8,128)(2,1)S(1)} %select_bitcast_fusion.bases, bf16[4,128,256]{2,1,0:T(8,128)(2,1)S(1)} %leaf.2.rest_0_.state), custom_call_target="tpu_custom_call" | custom-call | tf_op jit(solution)/shard_map/leaf/pallas_call | solution.py:72
  70.0 1.7 %collective-permute-start.2 = (bf16[4,128,256]{2,1,0:T(8,128)(2,1)S(1)}, bf16[4,128,256]{2,1,0:T(8,128)(2,1)S(1)}, u32[]{:S(2)}, u32[]{:S(2)}) collective-permute-start(bf16[4,128,256]{2,1,0:T(8,128)(2,1)S(1)} %get-tuple-element.16.state), channel_id=1, source_target_pairs={{0,8},{1,9},{2,10},{3,11},{4,12},{5,13},{6,14},{7,15},{8,0},{9,1},... | collective-permute-start | bytes 786440 | tf_op jit(solution)/shard_map/ppermute | solution.py:19
  71.8 1.9 %collective-permute-start.1 = (bf16[4,128,256]{2,1,0:T(8,128)(2,1)S(1)}, bf16[4,128,256]{2,1,0:T(8,128)(2,1)S(1)}, u32[]{:S(2)}, u32[]{:S(2)}) collective-permute-start(bf16[4,128,256]{2,1,0:T(8,128)(2,1)S(1)} %get-tuple-element.15.state), channel_id=1, source_target_pairs={{0,8},{1,9},{2,10},{3,11},{4,12},{5,13},{6,14},{7,15},{8,0},{9,1},... | collective-permute-start | bytes 786440 | tf_op jit(solution)/shard_map/ppermute | solution.py:19
  73.6 1.6 %collective-permute-start = (bf16[4,128,256]{2,1,0:T(8,128)(2,1)S(1)}, bf16[4,128,256]{2,1,0:T(8,128)(2,1)S(1)}, u32[]{:S(2)}, u32[]{:S(2)}) collective-permute-start(bf16[4,128,256]{2,1,0:T(8,128)(2,1)S(1)} %get-tuple-element.14.rest_0_.state), channel_id=1, source_target_pairs={{0,8},{1,9},{2,10},{3,11},{4,12},{5,13},{6,14},{7,15},{8,0},{9,1},... | collective-permute-start | bytes 786440 | tf_op jit(solution)/shard_map/ppermute | solution.py:19
  75.3 0.2 level.12.rest_0_.state
  75.5 0.7 collective-permute-start.7
  76.3 4.5 %collective-permute-done.2.other = bf16[4,128,256]{2,1,0:T(8,128)(2,1)S(1)} collective-permute-done((bf16[4,128,256]{2,1,0:T(8,128)(2,1)S(1)}, bf16[4,128,256]{2,1,0:T(8,128)(2,1)S(1)}, u32[]{:S(2)}, u32[]{:S(2)}) %collective-permute-start.2) | collective-permute-done | bytes 262176 | tf_op jit(solution)/shard_map/ppermute | solution.py:19
  80.8 0.2 level.13.rest_0_.state
  81.0 2.1 %collective-permute-start.6 = (bf16[4,128,256]{2,1,0:T(8,128)(2,1)S(1)}, bf16[4,128,256]{2,1,0:T(8,128)(2,1)S(1)}, u32[]{:S(2)}, u32[]{:S(2)}) collective-permute-start(bf16[4,128,256]{2,1,0:T(8,128)(2,1)S(1)} %level.13.rest_0_.state), channel_id=1, source_target_pairs={{0,4},{1,5},{2,6},{3,7},{4,0},{5,1},{6,2},{7,3},{8,12},{9,13},{10,... | collective-permute-start | bytes 786440 | tf_op jit(solution)/shard_map/ppermute | solution.py:19
  83.1 3.3 %collective-permute-done.1.other = bf16[4,128,256]{2,1,0:T(8,128)(2,1)S(1)} collective-permute-done((bf16[4,128,256]{2,1,0:T(8,128)(2,1)S(1)}, bf16[4,128,256]{2,1,0:T(8,128)(2,1)S(1)}, u32[]{:S(2)}, u32[]{:S(2)}) %collective-permute-start.1) | collective-permute-done | bytes 262176 | tf_op jit(solution)/shard_map/ppermute | solution.py:19
  86.4 0.2 level.14.rest_0_.state
  86.7 2.1 %collective-permute-start.5 = (bf16[4,128,256]{2,1,0:T(8,128)(2,1)S(1)}, bf16[4,128,256]{2,1,0:T(8,128)(2,1)S(1)}, u32[]{:S(2)}, u32[]{:S(2)}) collective-permute-start(bf16[4,128,256]{2,1,0:T(8,128)(2,1)S(1)} %level.14.rest_0_.state), channel_id=1, source_target_pairs={{0,4},{1,5},{2,6},{3,7},{4,0},{5,1},{6,2},{7,3},{8,12},{9,13},{10,... | collective-permute-start | bytes 786440 | tf_op jit(solution)/shard_map/ppermute | solution.py:19
  88.7 2.5 %collective-permute-done.other = bf16[4,128,256]{2,1,0:T(8,128)(2,1)S(1)} collective-permute-done((bf16[4,128,256]{2,1,0:T(8,128)(2,1)S(1)}, bf16[4,128,256]{2,1,0:T(8,128)(2,1)S(1)}, u32[]{:S(2)}, u32[]{:S(2)}) %collective-permute-start) | collective-permute-done | bytes 262176 | tf_op jit(solution)/shard_map/ppermute | solution.py:19
  91.3 0.2 level.15.rest_0_.state
  91.5 0.7 collective-permute-start.4
  92.2 0.2 level.16.rest_0_.state
  92.4 1.7 %collective-permute-start.11 = (bf16[4,128,256]{2,1,0:T(8,128)(2,1)S(1)}, bf16[4,128,256]{2,1,0:T(8,128)(2,1)S(1)}, u32[]{:S(2)}, u32[]{:S(2)}) collective-permute-start(bf16[4,128,256]{2,1,0:T(8,128)(2,1)S(1)} %level.16.rest_0_.state), channel_id=1, source_target_pairs={{0,2},{1,3},{2,0},{3,1},{4,6},{5,7},{6,4},{7,5},{8,10},{9,11},{10,... | collective-permute-start | bytes 786440 | tf_op jit(solution)/shard_map/ppermute | solution.py:19
  94.1 0.2 level.17.rest_0_.state
  94.3 0.5 collective-permute-start.10
  94.8 1.4 %collective-permute-done.5.other = bf16[4,128,256]{2,1,0:T(8,128)(2,1)S(1)} collective-permute-done((bf16[4,128,256]{2,1,0:T(8,128)(2,1)S(1)}, bf16[4,128,256]{2,1,0:T(8,128)(2,1)S(1)}, u32[]{:S(2)}, u32[]{:S(2)}) %collective-permute-start.5) | collective-permute-done | bytes 262176 | tf_op jit(solution)/shard_map/ppermute | solution.py:19
  96.3 0.2 level.18.rest_0_.state
  96.5 0.8 collective-permute-start.9
  97.4 5.0 %collective-permute-done.4.other = bf16[4,128,256]{2,1,0:T(8,128)(2,1)S(1)} collective-permute-done((bf16[4,128,256]{2,1,0:T(8,128)(2,1)S(1)}, bf16[4,128,256]{2,1,0:T(8,128)(2,1)S(1)}, u32[]{:S(2)}, u32[]{:S(2)}) %collective-permute-start.4) | collective-permute-done | bytes 262176 | tf_op jit(solution)/shard_map/ppermute | solution.py:19
  102.3 0.2 level.19.rest_0_.state
  102.6 0.8 collective-permute-start.8
  103.3 3.2 %collective-permute-done.11.other = bf16[4,128,256]{2,1,0:T(8,128)(2,1)S(1)} collective-permute-done((bf16[4,128,256]{2,1,0:T(8,128)(2,1)S(1)}, bf16[4,128,256]{2,1,0:T(8,128)(2,1)S(1)}, u32[]{:S(2)}, u32[]{:S(2)}) %collective-permute-start.11) | collective-permute-done | bytes 262176 | tf_op jit(solution)/shard_map/ppermute | solution.py:19
  106.5 0.2 level.20.rest_0_.state
  106.8 0.2 collective-permute-start.15
  107.0 5.1 %collective-permute-done.10.other = bf16[4,128,256]{2,1,0:T(8,128)(2,1)S(1)} collective-permute-done((bf16[4,128,256]{2,1,0:T(8,128)(2,1)S(1)}, bf16[4,128,256]{2,1,0:T(8,128)(2,1)S(1)}, u32[]{:S(2)}, u32[]{:S(2)}) %collective-permute-start.10) | collective-permute-done | bytes 262176 | tf_op jit(solution)/shard_map/ppermute | solution.py:19
  112.1 0.2 level.21.rest_0_.state
  112.4 0.2 collective-permute-start.14
  112.6 5.1 %collective-permute-done.9.other = bf16[4,128,256]{2,1,0:T(8,128)(2,1)S(1)} collective-permute-done((bf16[4,128,256]{2,1,0:T(8,128)(2,1)S(1)}, bf16[4,128,256]{2,1,0:T(8,128)(2,1)S(1)}, u32[]{:S(2)}, u32[]{:S(2)}) %collective-permute-start.9) | collective-permute-done | bytes 262176 | tf_op jit(solution)/shard_map/ppermute | solution.py:19
  118.2 4.3 %collective-permute-done.8.other = bf16[4,128,256]{2,1,0:T(8,128)(2,1)S(1)} collective-permute-done((bf16[4,128,256]{2,1,0:T(8,128)(2,1)S(1)}, bf16[4,128,256]{2,1,0:T(8,128)(2,1)S(1)}, u32[]{:S(2)}, u32[]{:S(2)}) %collective-permute-start.8) | collective-permute-done | bytes 262176 | tf_op jit(solution)/shard_map/ppermute | solution.py:19
  122.5 0.2 level.23.state
  122.9 1.6 %finish.4.rest_0_ = bf16[8192,256]{1,0:T(8,128)(2,1)} custom-call(bf16[4,16,128,256]{3,2,1,0:T(8,128)(2,1)S(1)} %copy-done, bf16[4,128,256]{2,1,0:T(8,128)(2,1)S(1)} %level.20.rest_0_.state, bf16[4,128,256]{2,1,0:T(8,128)(2,1)S(1)} %collective-permute-done.15.other, bf16[8192,128]{1,0:T(8,128)(2,1)S(1)} %copy-done.1), custom_call_target="tpu_custom_call" | custom-call | tf_op jit(solution)/shard_map/finish/pallas_call | solution.py:99
  124.5 1.6 %finish.5.rest_0_ = bf16[8192,256]{1,0:T(8,128)(2,1)} custom-call(bf16[4,16,128,256]{3,2,1,0:T(8,128)(2,1)S(1)} %copy-done, bf16[4,128,256]{2,1,0:T(8,128)(2,1)S(1)} %level.21.rest_0_.state, bf16[4,128,256]{2,1,0:T(8,128)(2,1)S(1)} %collective-permute-done.14.other, bf16[8192,128]{1,0:T(8,128)(2,1)S(1)} %copy-done.1, ...), custom_call_target="tpu_custom_call", output_to_operand_aliasing={{}: (4, {})} | custom-call | tf_op jit(solution)/shard_map/finish/pallas_call | solution.py:99
  126.2 1.6 %finish.6.rest_0_ = bf16[8192,256]{1,0:T(8,128)(2,1)} custom-call(bf16[4,16,128,256]{3,2,1,0:T(8,128)(2,1)S(1)} %copy-done, bf16[4,128,256]{2,1,0:T(8,128)(2,1)S(1)} %level.22.rest_0_.state, bf16[4,128,256]{2,1,0:T(8,128)(2,1)S(1)} %collective-permute-done.13.other, bf16[8192,128]{1,0:T(8,128)(2,1)S(1)} %copy-done.1, ...), custom_call_target="tpu_custom_call", output_to_operand_aliasing={{}: (4, {})} | custom-call | tf_op jit(solution)/shard_map/finish/pallas_call | solution.py:99
  127.8 4.0 %collective-permute-done.12.other = bf16[4,128,256]{2,1,0:T(8,128)(2,1)S(1)} collective-permute-done((bf16[4,128,256]{2,1,0:T(8,128)(2,1)S(1)}, bf16[4,128,256]{2,1,0:T(8,128)(2,1)S(1)}, u32[]{:S(2)}, u32[]{:S(2)}) %collective-permute-start.12) | collective-permute-done | bytes 262176 | tf_op jit(solution)/shard_map/ppermute | solution.py:19
  131.8 1.6 %finish.7 = bf16[8192,256]{1,0:T(8,128)(2,1)} custom-call(bf16[4,16,128,256]{3,2,1,0:T(8,128)(2,1)S(1)} %copy-done, bf16[4,128,256]{2,1,0:T(8,128)(2,1)S(1)} %level.23.state, bf16[4,128,256]{2,1,0:T(8,128)(2,1)S(1)} %collective-permute-done.12.other, bf16[8192,128]{1,0:T(8,128)(2,1)S(1)} %copy-done.1, ...), custom_call_target="tpu_custom_call", output_to_operand_aliasing={{}: (4, {})} | custom-call | tf_op jit(solution)/shard_map/finish/pallas_call | solution.py:99
  (22 shorter events, 0.8 us)
Async XLA Ops:
  0.0 11.0 %copy-start.5 = (s32[5,16]{1,0:T(8,128)S(1)}, s32[5,16]{1,0:T(8,128)}, u32[]{:S(2)}) copy-start(s32[5,16]{1,0:T(8,128)} %param.11) | copy-start | bytes 964
  0.0 11.1 %copy-start.4 = (bf16[8192,128]{1,0:T(8,128)(2,1)S(1)}, bf16[8192,128]{1,0:T(8,128)(2,1)}, u32[]{:S(2)}) copy-start(bf16[8192,128]{1,0:T(8,128)(2,1)} %param.7) | copy-start | bytes 6291460
  0.0 62.5 %all-to-all-start = ((bf16[128,64,256]{2,1,0:T(8,128)(2,1)}), bf16[128,64,256]{2,1,0:T(8,128)(2,1)}, u32[]{:S(2)}, u32[]{:S(2)}) async-start(bf16[128,64,256]{2,1,0:T(8,128)(2,1)} %bitcast.7), calls=%async_computation | async-start | bytes 8388608 | tf_op jit(solution)/shard_map/all_to_all | solution.py:113
  13.7 2.2 %copy-start.2 = (bf16[4,16,128,128]{3,2,1,0:T(8,128)(2,1)S(1)}, bf16[4,16,128,128]{3,2,1,0:T(8,128)(2,1)}, u32[]{:S(2)}) copy-start(bf16[4,16,128,128]{3,2,1,0:T(8,128)(2,1)} %param.9) | copy-start | bytes 6291460
  13.7 2.9 %copy-start.3 = (bf16[4,16,128,128]{3,2,1,0:T(8,128)(2,1)S(1)}, bf16[4,16,128,128]{3,2,1,0:T(8,128)(2,1)}, u32[]{:S(2)}) copy-start(bf16[4,16,128,128]{3,2,1,0:T(8,128)(2,1)} %param.8) | copy-start | bytes 6291460
  64.4 10.9 %copy-start = (bf16[4,16,128,256]{3,2,1,0:T(8,128)(2,1)S(1)}, bf16[4,16,128,256]{3,2,1,0:T(8,128)(2,1)}, u32[]{:S(2)}) copy-start(bf16[4,16,128,256]{3,2,1,0:T(8,128)(2,1)} %maximum_select_fusion.maps) | copy-start | bytes 12582916
  64.4 10.9 %collective-permute-start.3 = (bf16[4,128,256]{2,1,0:T(8,128)(2,1)S(1)}, bf16[4,128,256]{2,1,0:T(8,128)(2,1)S(1)}, u32[]{:S(2)}, u32[]{:S(2)}) collective-permute-start(bf16[4,128,256]{2,1,0:T(8,128)(2,1)S(1)} %leaf.2.rest_0_.state), channel_id=1, source_target_pairs={{0,8},{1,9},{2,10},{3,11},{4,12},{5,13},{6,14},{7,15},{8,0},{9,1},... | collective-permute-start | bytes 786440 | tf_op jit(solution)/shard_map/ppermute | solution.py:19
  70.0 10.8 %collective-permute-start.2 = (bf16[4,128,256]{2,1,0:T(8,128)(2,1)S(1)}, bf16[4,128,256]{2,1,0:T(8,128)(2,1)S(1)}, u32[]{:S(2)}, u32[]{:S(2)}) collective-permute-start(bf16[4,128,256]{2,1,0:T(8,128)(2,1)S(1)} %get-tuple-element.16.state), channel_id=1, source_target_pairs={{0,8},{1,9},{2,10},{3,11},{4,12},{5,13},{6,14},{7,15},{8,0},{9,1},... | collective-permute-start | bytes 786440 | tf_op jit(solution)/shard_map/ppermute | solution.py:19
  71.8 14.7 %collective-permute-start.1 = (bf16[4,128,256]{2,1,0:T(8,128)(2,1)S(1)}, bf16[4,128,256]{2,1,0:T(8,128)(2,1)S(1)}, u32[]{:S(2)}, u32[]{:S(2)}) collective-permute-start(bf16[4,128,256]{2,1,0:T(8,128)(2,1)S(1)} %get-tuple-element.15.state), channel_id=1, source_target_pairs={{0,8},{1,9},{2,10},{3,11},{4,12},{5,13},{6,14},{7,15},{8,0},{9,1},... | collective-permute-start | bytes 786440 | tf_op jit(solution)/shard_map/ppermute | solution.py:19
  73.6 17.6 %collective-permute-start = (bf16[4,128,256]{2,1,0:T(8,128)(2,1)S(1)}, bf16[4,128,256]{2,1,0:T(8,128)(2,1)S(1)}, u32[]{:S(2)}, u32[]{:S(2)}) collective-permute-start(bf16[4,128,256]{2,1,0:T(8,128)(2,1)S(1)} %get-tuple-element.14.rest_0_.state), channel_id=1, source_target_pairs={{0,8},{1,9},{2,10},{3,11},{4,12},{5,13},{6,14},{7,15},{8,0},{9,1},... | collective-permute-start | bytes 786440 | tf_op jit(solution)/shard_map/ppermute | solution.py:19
  75.5 16.6 %collective-permute-start.7 = (bf16[4,128,256]{2,1,0:T(8,128)(2,1)S(1)}, bf16[4,128,256]{2,1,0:T(8,128)(2,1)S(1)}, u32[]{:S(2)}, u32[]{:S(2)}) collective-permute-start(bf16[4,128,256]{2,1,0:T(8,128)(2,1)S(1)} %level.12.rest_0_.state), channel_id=1, source_target_pairs={{0,4},{1,5},{2,6},{3,7},{4,0},{5,1},{6,2},{7,3},{8,12},{9,13},{10,... | collective-permute-start | bytes 786440 | tf_op jit(solution)/shard_map/ppermute | solution.py:19
  81.0 13.1 %collective-permute-start.6 = (bf16[4,128,256]{2,1,0:T(8,128)(2,1)S(1)}, bf16[4,128,256]{2,1,0:T(8,128)(2,1)S(1)}, u32[]{:S(2)}, u32[]{:S(2)}) collective-permute-start(bf16[4,128,256]{2,1,0:T(8,128)(2,1)S(1)} %level.13.rest_0_.state), channel_id=1, source_target_pairs={{0,4},{1,5},{2,6},{3,7},{4,0},{5,1},{6,2},{7,3},{8,12},{9,13},{10,... | collective-permute-start | bytes 786440 | tf_op jit(solution)/shard_map/ppermute | solution.py:19
  86.7 9.6 %collective-permute-start.5 = (bf16[4,128,256]{2,1,0:T(8,128)(2,1)S(1)}, bf16[4,128,256]{2,1,0:T(8,128)(2,1)S(1)}, u32[]{:S(2)}, u32[]{:S(2)}) collective-permute-start(bf16[4,128,256]{2,1,0:T(8,128)(2,1)S(1)} %level.14.rest_0_.state), channel_id=1, source_target_pairs={{0,4},{1,5},{2,6},{3,7},{4,0},{5,1},{6,2},{7,3},{8,12},{9,13},{10,... | collective-permute-start | bytes 786440 | tf_op jit(solution)/shard_map/ppermute | solution.py:19
  91.5 10.8 %collective-permute-start.4 = (bf16[4,128,256]{2,1,0:T(8,128)(2,1)S(1)}, bf16[4,128,256]{2,1,0:T(8,128)(2,1)S(1)}, u32[]{:S(2)}, u32[]{:S(2)}) collective-permute-start(bf16[4,128,256]{2,1,0:T(8,128)(2,1)S(1)} %level.15.rest_0_.state), channel_id=1, source_target_pairs={{0,4},{1,5},{2,6},{3,7},{4,0},{5,1},{6,2},{7,3},{8,12},{9,13},{10,... | collective-permute-start | bytes 786440 | tf_op jit(solution)/shard_map/ppermute | solution.py:19
  92.4 14.1 %collective-permute-start.11 = (bf16[4,128,256]{2,1,0:T(8,128)(2,1)S(1)}, bf16[4,128,256]{2,1,0:T(8,128)(2,1)S(1)}, u32[]{:S(2)}, u32[]{:S(2)}) collective-permute-start(bf16[4,128,256]{2,1,0:T(8,128)(2,1)S(1)} %level.16.rest_0_.state), channel_id=1, source_target_pairs={{0,2},{1,3},{2,0},{3,1},{4,6},{5,7},{6,4},{7,5},{8,10},{9,11},{10,... | collective-permute-start | bytes 786440 | tf_op jit(solution)/shard_map/ppermute | solution.py:19
  94.3 17.8 %collective-permute-start.10 = (bf16[4,128,256]{2,1,0:T(8,128)(2,1)S(1)}, bf16[4,128,256]{2,1,0:T(8,128)(2,1)S(1)}, u32[]{:S(2)}, u32[]{:S(2)}) collective-permute-start(bf16[4,128,256]{2,1,0:T(8,128)(2,1)S(1)} %level.17.rest_0_.state), channel_id=1, source_target_pairs={{0,2},{1,3},{2,0},{3,1},{4,6},{5,7},{6,4},{7,5},{8,10},{9,11},{10,... | collective-permute-start | bytes 786440 | tf_op jit(solution)/shard_map/ppermute | solution.py:19
  96.5 21.2 %collective-permute-start.9 = (bf16[4,128,256]{2,1,0:T(8,128)(2,1)S(1)}, bf16[4,128,256]{2,1,0:T(8,128)(2,1)S(1)}, u32[]{:S(2)}, u32[]{:S(2)}) collective-permute-start(bf16[4,128,256]{2,1,0:T(8,128)(2,1)S(1)} %level.18.rest_0_.state), channel_id=1, source_target_pairs={{0,2},{1,3},{2,0},{3,1},{4,6},{5,7},{6,4},{7,5},{8,10},{9,11},{10,... | collective-permute-start | bytes 786440 | tf_op jit(solution)/shard_map/ppermute | solution.py:19
  102.6 20.0 %collective-permute-start.8 = (bf16[4,128,256]{2,1,0:T(8,128)(2,1)S(1)}, bf16[4,128,256]{2,1,0:T(8,128)(2,1)S(1)}, u32[]{:S(2)}, u32[]{:S(2)}) collective-permute-start(bf16[4,128,256]{2,1,0:T(8,128)(2,1)S(1)} %level.19.rest_0_.state), channel_id=1, source_target_pairs={{0,2},{1,3},{2,0},{3,1},{4,6},{5,7},{6,4},{7,5},{8,10},{9,11},{10,... | collective-permute-start | bytes 786440 | tf_op jit(solution)/shard_map/ppermute | solution.py:19
  106.8 16.1 %collective-permute-start.15 = (bf16[4,128,256]{2,1,0:T(8,128)(2,1)S(1)}, bf16[4,128,256]{2,1,0:T(8,128)(2,1)S(1)}, u32[]{:S(2)}, u32[]{:S(2)}) collective-permute-start(bf16[4,128,256]{2,1,0:T(8,128)(2,1)S(1)} %level.20.rest_0_.state), channel_id=1, source_target_pairs={{0,64},{16,80},{32,96},{48,112},{64,0},{80,16},{96,32},{112,48},{1... | collective-permute-start | bytes 786440 | tf_op jit(solution)/shard_map/ppermute | solution.py:19
  112.4 10.5 %copy-start.1 = (bf16[8192,128]{1,0:T(8,128)(2,1)S(1)}, bf16[8192,128]{1,0:T(8,128)(2,1)}, u32[]{:S(2)}) copy-start(bf16[8192,128]{1,0:T(8,128)(2,1)} %expand.7) | copy-start | bytes 6291460
  112.4 12.1 %collective-permute-start.14 = (bf16[4,128,256]{2,1,0:T(8,128)(2,1)S(1)}, bf16[4,128,256]{2,1,0:T(8,128)(2,1)S(1)}, u32[]{:S(2)}, u32[]{:S(2)}) collective-permute-start(bf16[4,128,256]{2,1,0:T(8,128)(2,1)S(1)} %level.21.rest_0_.state), channel_id=1, source_target_pairs={{0,64},{16,80},{32,96},{48,112},{64,0},{80,16},{96,32},{112,48},{1... | collective-permute-start | bytes 786440 | tf_op jit(solution)/shard_map/ppermute | solution.py:19
  118.0 8.2 %collective-permute-start.13 = (bf16[4,128,256]{2,1,0:T(8,128)(2,1)S(1)}, bf16[4,128,256]{2,1,0:T(8,128)(2,1)S(1)}, u32[]{:S(2)}, u32[]{:S(2)}) collective-permute-start(bf16[4,128,256]{2,1,0:T(8,128)(2,1)S(1)} %level.22.rest_0_.state), channel_id=1, source_target_pairs={{0,64},{16,80},{32,96},{48,112},{64,0},{80,16},{96,32},{112,48},{1... | collective-permute-start | bytes 786440 | tf_op jit(solution)/shard_map/ppermute | solution.py:19
  122.8 9.1 %collective-permute-start.12 = (bf16[4,128,256]{2,1,0:T(8,128)(2,1)S(1)}, bf16[4,128,256]{2,1,0:T(8,128)(2,1)S(1)}, u32[]{:S(2)}, u32[]{:S(2)}) collective-permute-start(bf16[4,128,256]{2,1,0:T(8,128)(2,1)S(1)} %level.23.state), channel_id=1, source_target_pairs={{0,64},{16,80},{32,96},{48,112},{64,0},{80,16},{96,32},{112,48},{1... | collective-permute-start | bytes 786440 | tf_op jit(solution)/shard_map/ppermute | solution.py:19

commit v3 on v2

--- a/solution.py
+++ b/solution.py
@@ -8,8 +8,8 @@
 from jax.sharding import PartitionSpec as P
 
 LEAF = 512
-GROUPS = [[4], [4, 4, 4]]
-SIZES = sum(GROUPS, [])
+LEAVES = [[4], [4, 4, 4]]
+SPLITS = [[[4], [4], [4], [4]]]*3
 VMEM = pl.BlockSpec(memory_space=pltpu.VMEM)
 ANY = pl.BlockSpec(memory_space=pl.ANY)
 
@@ -22,14 +22,13 @@
 def leaf_kernel(first, outs, moved, bases, *rest):
     held, arrived = rest[-2:]
     places = [(out, i) for out in rest[-2 - outs : -2] for i in range(out.shape[0])]
-    copies = []
-    for n in range(len(places)):
-        copy = pltpu.make_async_copy(moved.at[pl.ds((first + n) * LEAF, LEAF)], held.at[n], arrived.at[n])
-        copy.start()
-        copies.append(copy)
+    count = len(places)
+    copy = pltpu.make_async_copy(moved.at[pl.ds(first * LEAF, count * LEAF)], held, arrived)
+    copy.start()
+    copy.wait()
     for n, (out, i) in enumerate(places):
-        copies[n].wait()
-        out[i] = jnp.dot(bases[first + n], held[n], preferred_element_type=jnp.float32).astype(jnp.bfloat16)
+        rows = held[pl.ds(n * LEAF, LEAF), :]
+        out[i] = jnp.dot(bases[first + n], rows, preferred_element_type=jnp.float32).astype(jnp.bfloat16)
 
 
 def mixed(maps, state, other):
@@ -37,10 +36,10 @@
     return jnp.dot(maps, values, preferred_element_type=jnp.float32).astype(jnp.bfloat16)
 
 
-def level_kernel(level, first, maps, state, other, *rest):
-    out = rest[-1]
-    for i in range(state.shape[0]):
-        out[i] = mixed(maps[level - 1, first + i], state[i], other[i])
+def level_kernel(level, first, outs, maps, state, other, *rest):
+    places = [(out, i) for out in rest[-outs:] for i in range(out.shape[0])]
+    for n, (out, i) in enumerate(places):
+        out[i] = mixed(maps[level - 1, first + n], state[n], other[n])
 
 
 def last_kernel(level, first, maps, state, other, expand, *rest):
@@ -74,20 +73,20 @@
         out_shape=[jax.ShapeDtypeStruct((n, rank_max, rhs), jnp.bfloat16) for n in counts],
         in_specs=[ANY, VMEM] + [ANY] * len(after),
         out_specs=[VMEM] * len(counts),
-        scratch_shapes=[pltpu.VMEM((count, LEAF, rhs), jnp.bfloat16), pltpu.SemaphoreType.DMA((count,))],
+        scratch_shapes=[pltpu.VMEM((count * LEAF, rhs), jnp.bfloat16), pltpu.SemaphoreType.DMA],
         compiler_params=limit(24),
         cost_estimate=cost(2 * count * LEAF * rank_max * rhs, count * LEAF * rhs * 2),
         name="leaf",
     )(moved, bases, *after)
 
 
-def advance(state, other, maps, level, first, after):
+def advance(state, other, maps, level, first, counts, after):
     count, rank_max, rhs = state.shape
     return pl.pallas_call(
-        functools.partial(level_kernel, level, first),
-        out_shape=jax.ShapeDtypeStruct(state.shape, jnp.bfloat16),
+        functools.partial(level_kernel, level, first, len(counts)),
+        out_shape=[jax.ShapeDtypeStruct((n, rank_max, rhs), jnp.bfloat16) for n in counts],
         in_specs=[VMEM] * 3 + [ANY] * len(after),
-        out_specs=VMEM,
+        out_specs=[VMEM] * len(counts),
         compiler_params=limit(24),
         cost_estimate=cost(4 * count * rank_max * rank_max * rhs, count * rank_max * rhs * 2),
         name="level",
@@ -119,24 +118,24 @@
     col_bits = lax.axis_size("col").bit_length() - 1
     row_bits = lax.axis_size("row").bit_length() - 1
     pairs = [("col", col_bits - 1), ("col", col_bits - 2), ("col", col_bits - 3), ("row", row_bits - 1)]
-    chunks, first = [], 0
-    for count in SIZES:
-        chunks.append((first, count))
-        first += count
     states, last, first = [], [], 0
-    for counts in GROUPS:
+    for counts in LEAVES:
         states += project(moved, bases, first, counts, last)
         last = [states[-1]]
         first += sum(counts)
     for level in range(1, 4):
         others = [swapped(s, *pairs[level - 1]) for s in states]
-        for c, (first, _) in enumerate(chunks):
-            states[c] = advance(states[c], others[c], maps, level, first, last)
-            last = [states[c]]
+        made, first = [], 0
+        for counts, state, other in zip(SPLITS[level - 1], states, others):
+            made += advance(state, other, maps, level, first, counts, last)
+            last = [made[-1]]
+            first += sum(counts)
+        states = made
     others = [swapped(s, *pairs[3]) for s in states]
-    last = []
-    for (first, _), state, other in zip(chunks, states, others):
+    last, first = [], 0
+    for state, other in zip(states, others):
         last = [finish(state, other, maps, expand_bases, 4, first, last)]
+        first += state.shape[0]
     return last[0]
 
 

time: 134 us -> 134 us (level)
  waiting for transfers between devices: 81.7 us -> 83.7 us
  starting transfers between devices: 28.3 us -> 26.6 us
  Pallas kernels: 14.7 us -> 13.2 us
    ppermute x16, waiting for transfers between devices: 38.7 us -> 40.7 us  [swapped(): lax.ppermute(block, axis, [(i, i ^ 1 << apart) for i in range(count)])]
    ppermute x16, starting transfers between devices: 17.3 us -> 15.6 us  [swapped(): lax.ppermute(block, axis, [(i, i ^ 1 << apart) for i in range(count)])]
    pallas_call x2, Pallas kernels: 5.54 us -> 4.02 us  [project(): pl.pallas_call(functools.partial(leaf_kernel, first, len(counts)), out_sh...]
  transfers between devices with their start and end apart: 17 -> 17, of which waited for: 12 -> 13; matrix products, arithmetic and copies ran while one was open for 6% -> 6% of each run, Pallas kernels for 8% -> 8%
where the time goes in v3:
time: 134 us; the launch traced here: 132 us
  waiting for transfers between devices  83.7 us (62%)
  starting transfers between devices  26.6 us (20%)
  Pallas kernels  13.2 us (10%)
  other arithmetic  4.96 us (4%)
  local copies, waits for them, and re-layouts  3.55 us (3%)
    all_to_all x1, waiting for transfers between devices, on_device(): lax.all_to_all(points, ('row', 'col'), split_axis=0, concat_axis=0, tiled...  43 us
    ppermute x16, waiting for transfers between devices, swapped(): lax.ppermute(block, axis, [(i, i ^ 1 << apart) for i in range(count)])  40.7 us
    ppermute x16, starting transfers between devices, swapped(): lax.ppermute(block, axis, [(i, i ^ 1 << apart) for i in range(count)])  15.6 us
    all_to_all x1, starting transfers between devices, on_device(): lax.all_to_all(points, ('row', 'col'), split_axis=0, concat_axis=0, tiled...  11 us
    pallas_call x4, Pallas kernels, finish(): pl.pallas_call(functools.partial(last_kernel, level, first), out_shape=ja...  6.4 us
    pallas_call x2, Pallas kernels, project(): pl.pallas_call(functools.partial(leaf_kernel, first, len(counts)), out_sh...  4.02 us
    select_n x1, other arithmetic, on_device(): jnp.where(keep[1:], jnp.concatenate([own_maps, partner_maps], axis=3), 0)  2.97 us
    pallas_call x12, Pallas kernels, advance(): pl.pallas_call(functools.partial(level_kernel, level, first, len(counts))...  2.79 us
  transfers between devices with their start and end apart: 17, of which 13 were waited for; matrix products, arithmetic and copies ran while one was open for 6% of the time, Pallas kernels for 8%

profile of v3, /device:TPU:2, one launch (start us, length us, event | category | flops | bytes accessed | tf_op | source)
XLA Modules:
  0.0 132.3 jit_solution(17984826732218095819)
XLA Ops:
  0.0 11.0 %all-to-all-start = ((bf16[128,64,256]{2,1,0:T(8,128)(2,1)}), bf16[128,64,256]{2,1,0:T(8,128)(2,1)}, u32[]{:S(2)}, u32[]{:S(2)}) async-start(bf16[128,64,256]{2,1,0:T(8,128)(2,1)} %bitcast.7), calls=%async_computation | async-start | bytes 8388608 | tf_op jit(solution)/shard_map/all_to_all | solution.py:112
  11.1 2.6 %copy.10 = bf16[16,512,128]{1,2,0:T(8,128)(2,1)} copy(bf16[16,512,128]{2,1,0:T(8,128)(2,1)S(1)} %bitcast.8) | data formatting | bytes 4194304 | tf_op jit(solution)/shard_map/reshape | solution.py:115
  13.7 1.9 %select_bitcast_fusion.bases = bf16[16,128,512]{2,1,0:T(8,128)(2,1)S(1)} fusion(bf16[16,512,128]{1,2,0:T(8,128)(2,1)} %copy.10, pred[16,128]{1,0:T(8,128)(4,1)S(1)} %slice_bitcast_fusion), kind=kLoop, calls=%fused_computation.1 | loop fusion | flops 1048576 | bytes 4196352 | tf_op jit(solution)/shard_map/jit(_where)/select_n | solution.py:115
  15.6 0.3 copy-done.2
  15.9 0.6 copy-done.3
  16.6 3.0 %maximum_select_fusion.maps = bf16[4,16,128,256]{3,2,1,0:T(8,128)(2,1)} fusion(bf16[4,16,128,128]{3,2,1,0:T(8,128)(2,1)S(1)} %copy-done.2, bf16[4,16,128,128]{3,2,1,0:T(8,128)(2,1)S(1)} %copy-done.3, pred[4,16,128]{2,1,0:T(8,128)(4,1)S(1)} %slice.11), kind=kLoop, calls=%fused_computation | loop fusion | flops 10485760 | bytes 8396800 | tf_op jit(solution)/shard_map/jit(_where)/select_n | solution.py:116
  19.5 43.0 %all-to-all-done = bf16[128,64,256]{2,1,0:T(8,128)(2,1)} async-done(((bf16[128,64,256]{2,1,0:T(8,128)(2,1)}), bf16[128,64,256]{2,1,0:T(8,128)(2,1)}, u32[]{:S(2)}, u32[]{:S(2)}) %all-to-all-start) | async-done | bytes 4194336 | tf_op jit(solution)/shard_map/all_to_all | solution.py:112
  62.5 1.5 %leaf.2.rest_0_.state = bf16[4,128,256]{2,1,0:T(8,128)(2,1)S(1)} custom-call(bf16[8192,256]{1,0:T(8,128)(2,1)} %bitcast.1.moved, bf16[16,128,512]{2,1,0:T(8,128)(2,1)S(1)} %select_bitcast_fusion.bases), custom_call_target="tpu_custom_call" | custom-call | tf_op jit(solution)/shard_map/leaf/pallas_call | solution.py:71
  64.1 2.0 %collective-permute-start.3 = (bf16[4,128,256]{2,1,0:T(8,128)(2,1)S(1)}, bf16[4,128,256]{2,1,0:T(8,128)(2,1)S(1)}, u32[]{:S(2)}, u32[]{:S(2)}) collective-permute-start(bf16[4,128,256]{2,1,0:T(8,128)(2,1)S(1)} %leaf.2.rest_0_.state), channel_id=1, source_target_pairs={{0,8},{1,9},{2,10},{3,11},{4,12},{5,13},{6,14},{7,15},{8,0},{9,1},... | collective-permute-start | bytes 786440 | tf_op jit(solution)/shard_map/ppermute | solution.py:19
  66.0 2.5 %leaf.3 = (bf16[4,128,256]{2,1,0:T(8,128)(2,1)S(1)}, bf16[4,128,256]{2,1,0:T(8,128)(2,1)S(1)}, bf16[4,128,256]{2,1,0:T(8,128)(2,1)S(1)}) custom-call(bf16[8192,256]{1,0:T(8,128)(2,1)} %bitcast.1.moved, bf16[16,128,512]{2,1,0:T(8,128)(2,1)S(1)} %select_bitcast_fusion.bases, bf16[4,128,256]{2,1,0:T(8,128)(2,1)S(1)} %leaf.2.rest_0_.state), custom_call_target="tpu_custom_call" | custom-call | tf_op jit(solution)/shard_map/leaf/pallas_call | solution.py:71
  68.5 1.7 %collective-permute-start.2 = (bf16[4,128,256]{2,1,0:T(8,128)(2,1)S(1)}, bf16[4,128,256]{2,1,0:T(8,128)(2,1)S(1)}, u32[]{:S(2)}, u32[]{:S(2)}) collective-permute-start(bf16[4,128,256]{2,1,0:T(8,128)(2,1)S(1)} %get-tuple-element.16.state), channel_id=1, source_target_pairs={{0,8},{1,9},{2,10},{3,11},{4,12},{5,13},{6,14},{7,15},{8,0},{9,1},... | collective-permute-start | bytes 786440 | tf_op jit(solution)/shard_map/ppermute | solution.py:19
  70.2 1.9 %collective-permute-start.1 = (bf16[4,128,256]{2,1,0:T(8,128)(2,1)S(1)}, bf16[4,128,256]{2,1,0:T(8,128)(2,1)S(1)}, u32[]{:S(2)}, u32[]{:S(2)}) collective-permute-start(bf16[4,128,256]{2,1,0:T(8,128)(2,1)S(1)} %get-tuple-element.15.state), channel_id=1, source_target_pairs={{0,8},{1,9},{2,10},{3,11},{4,12},{5,13},{6,14},{7,15},{8,0},{9,1},... | collective-permute-start | bytes 786440 | tf_op jit(solution)/shard_map/ppermute | solution.py:19
  72.1 1.6 %collective-permute-start = (bf16[4,128,256]{2,1,0:T(8,128)(2,1)S(1)}, bf16[4,128,256]{2,1,0:T(8,128)(2,1)S(1)}, u32[]{:S(2)}, u32[]{:S(2)}) collective-permute-start(bf16[4,128,256]{2,1,0:T(8,128)(2,1)S(1)} %get-tuple-element.14.rest_0_.state), channel_id=1, source_target_pairs={{0,8},{1,9},{2,10},{3,11},{4,12},{5,13},{6,14},{7,15},{8,0},{9,1},... | collective-permute-start | bytes 786440 | tf_op jit(solution)/shard_map/ppermute | solution.py:19
  73.8 1.0 collective-permute-done.3.other
  74.8 0.2 level.12.rest_0_.state
  75.1 5.3 %collective-permute-done.2.other = bf16[4,128,256]{2,1,0:T(8,128)(2,1)S(1)} collective-permute-done((bf16[4,128,256]{2,1,0:T(8,128)(2,1)S(1)}, bf16[4,128,256]{2,1,0:T(8,128)(2,1)S(1)}, u32[]{:S(2)}, u32[]{:S(2)}) %collective-permute-start.2) | collective-permute-done | bytes 262176 | tf_op jit(solution)/shard_map/ppermute | solution.py:19
  80.4 0.2 level.13.rest_0_.state
  80.6 0.9 collective-permute-start.6
  81.6 4.4 %collective-permute-done.1.other = bf16[4,128,256]{2,1,0:T(8,128)(2,1)S(1)} collective-permute-done((bf16[4,128,256]{2,1,0:T(8,128)(2,1)S(1)}, bf16[4,128,256]{2,1,0:T(8,128)(2,1)S(1)}, u32[]{:S(2)}, u32[]{:S(2)}) %collective-permute-start.1) | collective-permute-done | bytes 262176 | tf_op jit(solution)/shard_map/ppermute | solution.py:19
  86.0 0.2 level.14.rest_0_.state
  86.3 0.9 collective-permute-start.5
  87.2 3.7 %collective-permute-done.other = bf16[4,128,256]{2,1,0:T(8,128)(2,1)S(1)} collective-permute-done((bf16[4,128,256]{2,1,0:T(8,128)(2,1)S(1)}, bf16[4,128,256]{2,1,0:T(8,128)(2,1)S(1)}, u32[]{:S(2)}, u32[]{:S(2)}) %collective-permute-start) | collective-permute-done | bytes 262176 | tf_op jit(solution)/shard_map/ppermute | solution.py:19
  90.9 0.2 level.15.rest_0_.state
  91.3 0.2 level.16.rest_0_.state
  91.5 1.6 %collective-permute-start.11 = (bf16[4,128,256]{2,1,0:T(8,128)(2,1)S(1)}, bf16[4,128,256]{2,1,0:T(8,128)(2,1)S(1)}, u32[]{:S(2)}, u32[]{:S(2)}) collective-permute-start(bf16[4,128,256]{2,1,0:T(8,128)(2,1)S(1)} %level.16.rest_0_.state), channel_id=1, source_target_pairs={{0,2},{1,3},{2,0},{3,1},{4,6},{5,7},{6,4},{7,5},{8,10},{9,11},{10,... | collective-permute-start | bytes 786440 | tf_op jit(solution)/shard_map/ppermute | solution.py:19
  93.1 0.2 level.17.rest_0_.state
  93.4 0.6 collective-permute-start.10
  94.0 0.8 collective-permute-done.5.other
  94.8 0.2 level.18.rest_0_.state
  95.0 0.8 collective-permute-start.9
  95.8 6.2 %collective-permute-done.4.other = bf16[4,128,256]{2,1,0:T(8,128)(2,1)S(1)} collective-permute-done((bf16[4,128,256]{2,1,0:T(8,128)(2,1)S(1)}, bf16[4,128,256]{2,1,0:T(8,128)(2,1)S(1)}, u32[]{:S(2)}, u32[]{:S(2)}) %collective-permute-start.4) | collective-permute-done | bytes 262176 | tf_op jit(solution)/shard_map/ppermute | solution.py:19
  102.0 0.2 level.19.rest_0_.state
  102.3 3.3 %collective-permute-done.11.other = bf16[4,128,256]{2,1,0:T(8,128)(2,1)S(1)} collective-permute-done((bf16[4,128,256]{2,1,0:T(8,128)(2,1)S(1)}, bf16[4,128,256]{2,1,0:T(8,128)(2,1)S(1)}, u32[]{:S(2)}, u32[]{:S(2)}) %collective-permute-start.11) | collective-permute-done | bytes 262176 | tf_op jit(solution)/shard_map/ppermute | solution.py:19
  105.6 0.2 level.20.rest_0_.state
  105.8 0.8 collective-permute-start.15
  106.6 4.6 %collective-permute-done.10.other = bf16[4,128,256]{2,1,0:T(8,128)(2,1)S(1)} collective-permute-done((bf16[4,128,256]{2,1,0:T(8,128)(2,1)S(1)}, bf16[4,128,256]{2,1,0:T(8,128)(2,1)S(1)}, u32[]{:S(2)}, u32[]{:S(2)}) %collective-permute-start.10) | collective-permute-done | bytes 262176 | tf_op jit(solution)/shard_map/ppermute | solution.py:19
  111.5 0.8 collective-permute-start.14
  112.3 4.6 %collective-permute-done.9.other = bf16[4,128,256]{2,1,0:T(8,128)(2,1)S(1)} collective-permute-done((bf16[4,128,256]{2,1,0:T(8,128)(2,1)S(1)}, bf16[4,128,256]{2,1,0:T(8,128)(2,1)S(1)}, u32[]{:S(2)}, u32[]{:S(2)}) %collective-permute-start.9) | collective-permute-done | bytes 262176 | tf_op jit(solution)/shard_map/ppermute | solution.py:19
  117.1 0.8 collective-permute-start.13
  117.9 3.2 %collective-permute-done.8.other = bf16[4,128,256]{2,1,0:T(8,128)(2,1)S(1)} collective-permute-done((bf16[4,128,256]{2,1,0:T(8,128)(2,1)S(1)}, bf16[4,128,256]{2,1,0:T(8,128)(2,1)S(1)}, u32[]{:S(2)}, u32[]{:S(2)}) %collective-permute-start.8) | collective-permute-done | bytes 262176 | tf_op jit(solution)/shard_map/ppermute | solution.py:19
  121.1 0.2 level.23.state
  121.3 1.0 collective-permute-start.12
  122.3 1.6 %finish.4.rest_0_ = bf16[8192,256]{1,0:T(8,128)(2,1)} custom-call(bf16[4,16,128,256]{3,2,1,0:T(8,128)(2,1)S(1)} %copy-done, bf16[4,128,256]{2,1,0:T(8,128)(2,1)S(1)} %level.20.rest_0_.state, bf16[4,128,256]{2,1,0:T(8,128)(2,1)S(1)} %collective-permute-done.15.other, bf16[8192,128]{1,0:T(8,128)(2,1)S(1)} %copy-done.1), custom_call_target="tpu_custom_call" | custom-call | tf_op jit(solution)/shard_map/finish/pallas_call | solution.py:98
  123.9 1.6 %finish.5.rest_0_ = bf16[8192,256]{1,0:T(8,128)(2,1)} custom-call(bf16[4,16,128,256]{3,2,1,0:T(8,128)(2,1)S(1)} %copy-done, bf16[4,128,256]{2,1,0:T(8,128)(2,1)S(1)} %level.21.rest_0_.state, bf16[4,128,256]{2,1,0:T(8,128)(2,1)S(1)} %collective-permute-done.14.other, bf16[8192,128]{1,0:T(8,128)(2,1)S(1)} %copy-done.1, ...), custom_call_target="tpu_custom_call", output_to_operand_aliasing={{}: (4, {})} | custom-call | tf_op jit(solution)/shard_map/finish/pallas_call | solution.py:98
  125.5 0.3 collective-permute-done.13.other
  125.8 1.6 %finish.6.rest_0_ = bf16[8192,256]{1,0:T(8,128)(2,1)} custom-call(bf16[4,16,128,256]{3,2,1,0:T(8,128)(2,1)S(1)} %copy-done, bf16[4,128,256]{2,1,0:T(8,128)(2,1)S(1)} %level.22.rest_0_.state, bf16[4,128,256]{2,1,0:T(8,128)(2,1)S(1)} %collective-permute-done.13.other, bf16[8192,128]{1,0:T(8,128)(2,1)S(1)} %copy-done.1, ...), custom_call_target="tpu_custom_call", output_to_operand_aliasing={{}: (4, {})} | custom-call | tf_op jit(solution)/shard_map/finish/pallas_call | solution.py:98
  127.4 3.3 %collective-permute-done.12.other = bf16[4,128,256]{2,1,0:T(8,128)(2,1)S(1)} collective-permute-done((bf16[4,128,256]{2,1,0:T(8,128)(2,1)S(1)}, bf16[4,128,256]{2,1,0:T(8,128)(2,1)S(1)}, u32[]{:S(2)}, u32[]{:S(2)}) %collective-permute-start.12) | collective-permute-done | bytes 262176 | tf_op jit(solution)/shard_map/ppermute | solution.py:19
  130.7 1.6 %finish.7 = bf16[8192,256]{1,0:T(8,128)(2,1)} custom-call(bf16[4,16,128,256]{3,2,1,0:T(8,128)(2,1)S(1)} %copy-done, bf16[4,128,256]{2,1,0:T(8,128)(2,1)S(1)} %level.23.state, bf16[4,128,256]{2,1,0:T(8,128)(2,1)S(1)} %collective-permute-done.12.other, bf16[8192,128]{1,0:T(8,128)(2,1)S(1)} %copy-done.1, ...), custom_call_target="tpu_custom_call", output_to_operand_aliasing={{}: (4, {})} | custom-call | tf_op jit(solution)/shard_map/finish/pallas_call | solution.py:98
  (22 shorter events, 0.8 us)
Async XLA Ops:
  0.0 11.0 %copy-start.5 = (s32[5,16]{1,0:T(8,128)S(1)}, s32[5,16]{1,0:T(8,128)}, u32[]{:S(2)}) copy-start(s32[5,16]{1,0:T(8,128)} %param.11) | copy-start | bytes 964
  0.0 11.1 %copy-start.4 = (bf16[8192,128]{1,0:T(8,128)(2,1)S(1)}, bf16[8192,128]{1,0:T(8,128)(2,1)}, u32[]{:S(2)}) copy-start(bf16[8192,128]{1,0:T(8,128)(2,1)} %param.7) | copy-start | bytes 6291460
  0.0 62.5 %all-to-all-start = ((bf16[128,64,256]{2,1,0:T(8,128)(2,1)}), bf16[128,64,256]{2,1,0:T(8,128)(2,1)}, u32[]{:S(2)}, u32[]{:S(2)}) async-start(bf16[128,64,256]{2,1,0:T(8,128)(2,1)} %bitcast.7), calls=%async_computation | async-start | bytes 8388608 | tf_op jit(solution)/shard_map/all_to_all | solution.py:112
  13.7 2.2 %copy-start.2 = (bf16[4,16,128,128]{3,2,1,0:T(8,128)(2,1)S(1)}, bf16[4,16,128,128]{3,2,1,0:T(8,128)(2,1)}, u32[]{:S(2)}) copy-start(bf16[4,16,128,128]{3,2,1,0:T(8,128)(2,1)} %param.9) | copy-start | bytes 6291460
  13.7 2.9 %copy-start.3 = (bf16[4,16,128,128]{3,2,1,0:T(8,128)(2,1)S(1)}, bf16[4,16,128,128]{3,2,1,0:T(8,128)(2,1)}, u32[]{:S(2)}) copy-start(bf16[4,16,128,128]{3,2,1,0:T(8,128)(2,1)} %param.8) | copy-start | bytes 6291460
  64.1 10.7 %copy-start = (bf16[4,16,128,256]{3,2,1,0:T(8,128)(2,1)S(1)}, bf16[4,16,128,256]{3,2,1,0:T(8,128)(2,1)}, u32[]{:S(2)}) copy-start(bf16[4,16,128,256]{3,2,1,0:T(8,128)(2,1)} %maximum_select_fusion.maps) | copy-start | bytes 12582916
  64.1 10.7 %collective-permute-start.3 = (bf16[4,128,256]{2,1,0:T(8,128)(2,1)S(1)}, bf16[4,128,256]{2,1,0:T(8,128)(2,1)S(1)}, u32[]{:S(2)}, u32[]{:S(2)}) collective-permute-start(bf16[4,128,256]{2,1,0:T(8,128)(2,1)S(1)} %leaf.2.rest_0_.state), channel_id=1, source_target_pairs={{0,8},{1,9},{2,10},{3,11},{4,12},{5,13},{6,14},{7,15},{8,0},{9,1},... | collective-permute-start | bytes 786440 | tf_op jit(solution)/shard_map/ppermute | solution.py:19
  68.5 11.9 %collective-permute-start.2 = (bf16[4,128,256]{2,1,0:T(8,128)(2,1)S(1)}, bf16[4,128,256]{2,1,0:T(8,128)(2,1)S(1)}, u32[]{:S(2)}, u32[]{:S(2)}) collective-permute-start(bf16[4,128,256]{2,1,0:T(8,128)(2,1)S(1)} %get-tuple-element.16.state), channel_id=1, source_target_pairs={{0,8},{1,9},{2,10},{3,11},{4,12},{5,13},{6,14},{7,15},{8,0},{9,1},... | collective-permute-start | bytes 786440 | tf_op jit(solution)/shard_map/ppermute | solution.py:19
  70.2 15.8 %collective-permute-start.1 = (bf16[4,128,256]{2,1,0:T(8,128)(2,1)S(1)}, bf16[4,128,256]{2,1,0:T(8,128)(2,1)S(1)}, u32[]{:S(2)}, u32[]{:S(2)}) collective-permute-start(bf16[4,128,256]{2,1,0:T(8,128)(2,1)S(1)} %get-tuple-element.15.state), channel_id=1, source_target_pairs={{0,8},{1,9},{2,10},{3,11},{4,12},{5,13},{6,14},{7,15},{8,0},{9,1},... | collective-permute-start | bytes 786440 | tf_op jit(solution)/shard_map/ppermute | solution.py:19
  72.1 18.8 %collective-permute-start = (bf16[4,128,256]{2,1,0:T(8,128)(2,1)S(1)}, bf16[4,128,256]{2,1,0:T(8,128)(2,1)S(1)}, u32[]{:S(2)}, u32[]{:S(2)}) collective-permute-start(bf16[4,128,256]{2,1,0:T(8,128)(2,1)S(1)} %get-tuple-element.14.rest_0_.state), channel_id=1, source_target_pairs={{0,8},{1,9},{2,10},{3,11},{4,12},{5,13},{6,14},{7,15},{8,0},{9,1},... | collective-permute-start | bytes 786440 | tf_op jit(solution)/shard_map/ppermute | solution.py:19
  75.0 16.2 %collective-permute-start.7 = (bf16[4,128,256]{2,1,0:T(8,128)(2,1)S(1)}, bf16[4,128,256]{2,1,0:T(8,128)(2,1)S(1)}, u32[]{:S(2)}, u32[]{:S(2)}) collective-permute-start(bf16[4,128,256]{2,1,0:T(8,128)(2,1)S(1)} %level.12.rest_0_.state), channel_id=1, source_target_pairs={{0,4},{1,5},{2,6},{3,7},{4,0},{5,1},{6,2},{7,3},{8,12},{9,13},{10,... | collective-permute-start | bytes 786440 | tf_op jit(solution)/shard_map/ppermute | solution.py:19
  80.6 12.5 %collective-permute-start.6 = (bf16[4,128,256]{2,1,0:T(8,128)(2,1)S(1)}, bf16[4,128,256]{2,1,0:T(8,128)(2,1)S(1)}, u32[]{:S(2)}, u32[]{:S(2)}) collective-permute-start(bf16[4,128,256]{2,1,0:T(8,128)(2,1)S(1)} %level.13.rest_0_.state), channel_id=1, source_target_pairs={{0,4},{1,5},{2,6},{3,7},{4,0},{5,1},{6,2},{7,3},{8,12},{9,13},{10,... | collective-permute-start | bytes 786440 | tf_op jit(solution)/shard_map/ppermute | solution.py:19
  86.3 8.5 %collective-permute-start.5 = (bf16[4,128,256]{2,1,0:T(8,128)(2,1)S(1)}, bf16[4,128,256]{2,1,0:T(8,128)(2,1)S(1)}, u32[]{:S(2)}, u32[]{:S(2)}) collective-permute-start(bf16[4,128,256]{2,1,0:T(8,128)(2,1)S(1)} %level.14.rest_0_.state), channel_id=1, source_target_pairs={{0,4},{1,5},{2,6},{3,7},{4,0},{5,1},{6,2},{7,3},{8,12},{9,13},{10,... | collective-permute-start | bytes 786440 | tf_op jit(solution)/shard_map/ppermute | solution.py:19
  91.2 10.8 %collective-permute-start.4 = (bf16[4,128,256]{2,1,0:T(8,128)(2,1)S(1)}, bf16[4,128,256]{2,1,0:T(8,128)(2,1)S(1)}, u32[]{:S(2)}, u32[]{:S(2)}) collective-permute-start(bf16[4,128,256]{2,1,0:T(8,128)(2,1)S(1)} %level.15.rest_0_.state), channel_id=1, source_target_pairs={{0,4},{1,5},{2,6},{3,7},{4,0},{5,1},{6,2},{7,3},{8,12},{9,13},{10,... | collective-permute-start | bytes 786440 | tf_op jit(solution)/shard_map/ppermute | solution.py:19
  91.5 14.1 %collective-permute-start.11 = (bf16[4,128,256]{2,1,0:T(8,128)(2,1)S(1)}, bf16[4,128,256]{2,1,0:T(8,128)(2,1)S(1)}, u32[]{:S(2)}, u32[]{:S(2)}) collective-permute-start(bf16[4,128,256]{2,1,0:T(8,128)(2,1)S(1)} %level.16.rest_0_.state), channel_id=1, source_target_pairs={{0,2},{1,3},{2,0},{3,1},{4,6},{5,7},{6,4},{7,5},{8,10},{9,11},{10,... | collective-permute-start | bytes 786440 | tf_op jit(solution)/shard_map/ppermute | solution.py:19
  93.4 17.9 %collective-permute-start.10 = (bf16[4,128,256]{2,1,0:T(8,128)(2,1)S(1)}, bf16[4,128,256]{2,1,0:T(8,128)(2,1)S(1)}, u32[]{:S(2)}, u32[]{:S(2)}) collective-permute-start(bf16[4,128,256]{2,1,0:T(8,128)(2,1)S(1)} %level.17.rest_0_.state), channel_id=1, source_target_pairs={{0,2},{1,3},{2,0},{3,1},{4,6},{5,7},{6,4},{7,5},{8,10},{9,11},{10,... | collective-permute-start | bytes 786440 | tf_op jit(solution)/shard_map/ppermute | solution.py:19
  95.0 21.8 %collective-permute-start.9 = (bf16[4,128,256]{2,1,0:T(8,128)(2,1)S(1)}, bf16[4,128,256]{2,1,0:T(8,128)(2,1)S(1)}, u32[]{:S(2)}, u32[]{:S(2)}) collective-permute-start(bf16[4,128,256]{2,1,0:T(8,128)(2,1)S(1)} %level.18.rest_0_.state), channel_id=1, source_target_pairs={{0,2},{1,3},{2,0},{3,1},{4,6},{5,7},{6,4},{7,5},{8,10},{9,11},{10,... | collective-permute-start | bytes 786440 | tf_op jit(solution)/shard_map/ppermute | solution.py:19
  102.3 18.8 %collective-permute-start.8 = (bf16[4,128,256]{2,1,0:T(8,128)(2,1)S(1)}, bf16[4,128,256]{2,1,0:T(8,128)(2,1)S(1)}, u32[]{:S(2)}, u32[]{:S(2)}) collective-permute-start(bf16[4,128,256]{2,1,0:T(8,128)(2,1)S(1)} %level.19.rest_0_.state), channel_id=1, source_target_pairs={{0,2},{1,3},{2,0},{3,1},{4,6},{5,7},{6,4},{7,5},{8,10},{9,11},{10,... | collective-permute-start | bytes 786440 | tf_op jit(solution)/shard_map/ppermute | solution.py:19
  105.8 16.4 %collective-permute-start.15 = (bf16[4,128,256]{2,1,0:T(8,128)(2,1)S(1)}, bf16[4,128,256]{2,1,0:T(8,128)(2,1)S(1)}, u32[]{:S(2)}, u32[]{:S(2)}) collective-permute-start(bf16[4,128,256]{2,1,0:T(8,128)(2,1)S(1)} %level.20.rest_0_.state), channel_id=1, source_target_pairs={{0,64},{16,80},{32,96},{48,112},{64,0},{80,16},{96,32},{112,48},{1... | collective-permute-start | bytes 786440 | tf_op jit(solution)/shard_map/ppermute | solution.py:19
  111.5 10.8 %copy-start.1 = (bf16[8192,128]{1,0:T(8,128)(2,1)S(1)}, bf16[8192,128]{1,0:T(8,128)(2,1)}, u32[]{:S(2)}) copy-start(bf16[8192,128]{1,0:T(8,128)(2,1)} %expand.7) | copy-start | bytes 6291460
  111.5 12.4 %collective-permute-start.14 = (bf16[4,128,256]{2,1,0:T(8,128)(2,1)S(1)}, bf16[4,128,256]{2,1,0:T(8,128)(2,1)S(1)}, u32[]{:S(2)}, u32[]{:S(2)}) collective-permute-start(bf16[4,128,256]{2,1,0:T(8,128)(2,1)S(1)} %level.21.rest_0_.state), channel_id=1, source_target_pairs={{0,64},{16,80},{32,96},{48,112},{64,0},{80,16},{96,32},{112,48},{1... | collective-permute-start | bytes 786440 | tf_op jit(solution)/shard_map/ppermute | solution.py:19
  117.1 8.7 %collective-permute-start.13 = (bf16[4,128,256]{2,1,0:T(8,128)(2,1)S(1)}, bf16[4,128,256]{2,1,0:T(8,128)(2,1)S(1)}, u32[]{:S(2)}, u32[]{:S(2)}) collective-permute-start(bf16[4,128,256]{2,1,0:T(8,128)(2,1)S(1)} %level.22.rest_0_.state), channel_id=1, source_target_pairs={{0,64},{16,80},{32,96},{48,112},{64,0},{80,16},{96,32},{112,48},{1... | collective-permute-start | bytes 786440 | tf_op jit(solution)/shard_map/ppermute | solution.py:19
  121.3 9.3 %collective-permute-start.12 = (bf16[4,128,256]{2,1,0:T(8,128)(2,1)S(1)}, bf16[4,128,256]{2,1,0:T(8,128)(2,1)S(1)}, u32[]{:S(2)}, u32[]{:S(2)}) collective-permute-start(bf16[4,128,256]{2,1,0:T(8,128)(2,1)S(1)} %level.23.state), channel_id=1, source_target_pairs={{0,64},{16,80},{32,96},{48,112},{64,0},{80,16},{96,32},{112,48},{1... | collective-permute-start | bytes 786440 | tf_op jit(solution)/shard_map/ppermute | solution.py:19
